TPU v7x, 128 devices: a whole 4x4x4 slice. The times are simulated.
128 devices in a mesh: row: 16 (over x, y_hi, core), col: 8 (over z, y_lo).
Axes of the slice: x: 4, y: 4 (y_hi: 2, y_lo: 2; y = y_hi * 2 + y_lo), z: 4, core: 2. Of those that a mesh axis runs over, the one named last changes fastest.
Arguments:
- features: bfloat16 [131072, 128], P(('row', 'col')), may hold values from -6 to 6
- weight: bfloat16 [128, 128], replicated, may hold values from -0.5 to 0.5
- layer_bias: float32 [128], replicated, may hold values from -3 to 3
- cotangent: bfloat16 [131072, 128], P(('col', 'row')), may hold values from -6 to 6
- tile_out: int32 [16, 8, 128], P('row', 'col'), may hold values from 0 to 63
- tile_in: int32 [16, 8, 128], P('row', 'col'), may hold values from 0 to 31
- tile_vals: bfloat16 [16, 8, 128, 256, 256], P('row', 'col'), may hold values from -0.09375 to 0.09375
- tile_count: int32 [16, 8], P('row', 'col'), may hold values from 1 to 128, as said below
Outputs:
- hidden_out: bfloat16 [131072, 128], P(('col', 'row'))
- feature_grad: bfloat16 [131072, 128], P(('row', 'col'))
- weight_grad: float32 [128, 128], replicated
- bias_grad: float32 [128], replicated
Inputs may be any that keep to these rules, and one draw needn't show every extreme that they name: `tile_count`: live slots of each grid block; some grid block has exactly 128 in every draw.
All inputs are finite; a program needn't handle non-finite values.
Results may differ from a plain program's by a relative error of at most 0.025.
Values may be sent and summed in bfloat16 or wider, within the bound.
No kernel may reach another device: no remote copies, remote signals or barrier semaphores. Data moves between devices by JAX's collectives and lax.ppermute only.
A program may use at most 192 MiB of HBM per device.

v0:
```python
import functools
import math

import jax
import jax.numpy as jnp
from jax import lax
from jax.experimental import pallas as pl
from jax.experimental.pallas import tpu as pltpu
from jax.sharding import PartitionSpec as P

gelu_coef = 0.7978845608
cube_coef = 0.044715
TILE = 256
FEAT = 128
SLOTS = 128
NPEER = 8
LIST = 160
UNROLL = 8
DEPTH = 32
FWD_DUMMY = 32
BWD_DUMMY = 32
f32, bf16 = jnp.float32, jnp.bfloat16
VMEM_LIMIT = 28 * 2**20


def params():
    return pltpu.CompilerParams(vmem_limit_bytes=VMEM_LIMIT)


def vmem():
    return pl.BlockSpec(memory_space=pltpu.VMEM)


def smem():
    return pl.BlockSpec(memory_space=pltpu.SMEM)


def hbm():
    return pl.BlockSpec(memory_space=pl.ANY)


def prep_kernel(where_ref, out_ref, in_ref, count_ref, lists_ref):
    core = where_ref[0]

    def clear(i, carry):
        lists_ref[i] = FWD_DUMMY << 16
        lists_ref[LIST + i] = FWD_DUMMY << 16
        lists_ref[2 * LIST + i] = BWD_DUMMY << 16
        lists_ref[3 * LIST + i] = BWD_DUMMY << 16
        return carry

    lax.fori_loop(0, LIST, clear, 0)

    def place(k, carry):
        f0, f1 = carry
        t = out_ref[k]
        s = in_ref[k]
        rel = jnp.bitwise_xor((t >> 2) & 1, core)
        to_t = ((t >> 3) << 2) | (t & 3)
        at_f = jnp.where(rel == 0, f0, LIST + f1)
        lists_ref[at_f] = k | (s << 8) | (to_t << 16)
        lists_ref[2 * LIST + at_f] = k | (to_t << 8) | (s << 16)
        return (f0 + 1 - rel, f1 + rel)

    zero = jnp.int32(0)
    sizes = lax.fori_loop(0, count_ref[0], place, (zero, zero))
    lists_ref[4 * LIST] = sizes[0]
    lists_ref[4 * LIST + 1] = sizes[1]


def prep(where, out_index, in_index, count):
    return pl.pallas_call(
        prep_kernel,
        out_shape=jax.ShapeDtypeStruct((1024,), jnp.int32),
        in_specs=[smem()] * 4,
        out_specs=smem(),
        compiler_params=params(),
        name="slot_lists",
    )(where, out_index, in_index, count)


def copies_kernel(value_ref, out_ref, sems):
    copies = [
        pltpu.make_async_copy(value_ref, out_ref.at[peer], sems.at[peer]) for peer in range(NPEER)
    ]
    for copy in copies:
        copy.start()
    for copy in copies:
        copy.wait()


def copies_of(value):
    return pl.pallas_call(
        copies_kernel,
        out_shape=pltpu.HBM((NPEER, *value.shape), value.dtype),
        in_specs=[hbm()],
        out_specs=hbm(),
        scratch_shapes=[pltpu.SemaphoreType.DMA((NPEER,))],
        compiler_params=params(),
        name="copies",
    )(in_hbm(value))


def tile_loop(which, lists_ref, vals, buf, sems, acc, ready, product):
    base = which * LIST
    groups = (lists_ref[4 * LIST + (which & 1)] + (UNROLL - 1)) // UNROLL
    ahead = DEPTH // UNROLL

    def copy(g, u):
        slot = lists_ref[base + g * UNROLL + u] & 255
        at = lax.rem(g, ahead) * UNROLL + u
        return pltpu.make_async_copy(vals.at[slot], buf.at[at], sems.at[at])

    for g in range(ahead):

        @pl.when(g < groups)
        def _():
            for u in range(UNROLL):
                copy(g, u).start()

    ready()

    def body(g, carry):
        for u in range(UNROLL):
            copy(g, u).wait()
        todo = []
        for u in range(UNROLL):
            entry = lists_ref[base + g * UNROLL + u]
            at = lax.rem(g, ahead) * UNROLL + u
            todo.append((entry >> 16, product(buf[at], (entry >> 8) & 255)))
        for to, value in todo:
            acc[to] += value

        @pl.when(g + ahead < groups)
        def _():
            for u in range(UNROLL):
                copy(g + ahead, u).start()

        return carry

    lax.fori_loop(0, groups, body, 0)


def in_hbm(array):
    return pltpu.with_memory_space_constraint(array, pltpu.HBM)


TILES_COST = pl.CostEstimate(
    flops=2 * 64 * TILE * TILE * FEAT, bytes_accessed=16 * 2**20, transcendentals=0
)


def forward_kernel(which, lists_ref, vals, x, out_ref, buf, acc, sems):
    def ready():
        def clear(i, carry):
            acc[i] = jnp.zeros((TILE, FEAT), f32)
            return carry

        lax.fori_loop(0, FWD_DUMMY, clear, 0)

    def product(tile, source):
        rows = pl.ds(pl.multiple_of((source & 3) * TILE, TILE), TILE)
        return jnp.dot(tile, x[source >> 2, rows, :], preferred_element_type=f32)

    tile_loop(which, lists_ref, vals, buf, sems, acc, ready, product)

    for i in range(4 * NPEER):
        out_ref[i // 4, pl.ds((i % 4) * TILE, TILE), :] = acc[i].astype(bf16)


def forward(which, lists, values, sources):
    return pl.pallas_call(
        functools.partial(forward_kernel, which),
        out_shape=jax.ShapeDtypeStruct((NPEER, 4 * TILE, FEAT), bf16),
        in_specs=[smem(), hbm(), vmem()],
        out_specs=vmem(),
        scratch_shapes=[
            pltpu.VMEM((DEPTH, TILE, TILE), bf16),
            pltpu.VMEM((FWD_DUMMY + 1, TILE, FEAT), f32),
            pltpu.SemaphoreType.DMA((DEPTH,)),
        ],
        compiler_params=params(),
        cost_estimate=TILES_COST,
        name="forward_tiles",
    )(in_hbm(lists), in_hbm(values), sources)


def pair_sum_kernel(mine_ref, other_ref, out_ref):
    for k in range(NPEER):
        out_ref[k] = (mine_ref[k].astype(f32) + other_ref[k].astype(f32)).astype(bf16)


def pair_sum(mine, other):
    return pl.pallas_call(
        pair_sum_kernel,
        out_shape=jax.ShapeDtypeStruct(mine.shape, bf16),
        in_specs=[vmem()] * 2,
        out_specs=vmem(),
        compiler_params=params(),
        cost_estimate=pl.CostEstimate(flops=2**21, bytes_accessed=6 * 2**20, transcendentals=0),
        name="pair_sum",
    )(mine, other)


def backward_kernel(which, lists_ref, vals, g, *rest):
    if which == 2:
        out, buf, acc, sems = rest
    else:
        before, out_ref, buf, acc, sems, out, out_sems = rest

    def ready():
        def clear(i, carry):
            acc[i] = jnp.zeros((FEAT, TILE), f32)
            return carry

        lax.fori_loop(0, BWD_DUMMY, clear, 0)

    def product(tile, source):
        rows = pl.ds(pl.multiple_of((source & 3) * FEAT, FEAT), FEAT)
        return jnp.dot(g[source >> 2, rows, :], tile, preferred_element_type=f32)

    tile_loop(which, lists_ref, vals, buf, sems, acc, ready, product)

    copies = []
    for i in range(4 * NPEER):
        peer, rows = i // 4, pl.ds((i % 4) * FEAT, FEAT)
        if which == 2:
            out[peer, rows, :] = acc[i].astype(bf16)
        else:
            out[peer, rows, :] = (acc[i] + before[peer, rows, :].astype(f32)).astype(bf16)
            if i % 4 == 3:
                copies.append(
                    pltpu.make_async_copy(out.at[peer], out_ref.at[peer], out_sems.at[peer])
                )
                copies[-1].start()
    for copy in copies:
        copy.wait()


def backward(which, lists, values, *blocks):
    shape = (NPEER, 4 * FEAT, TILE)
    scratch = [
        pltpu.VMEM((DEPTH, TILE, TILE), bf16),
        pltpu.VMEM((BWD_DUMMY + 1, FEAT, TILE), f32),
        pltpu.SemaphoreType.DMA((DEPTH,)),
    ]
    if which == 3:
        scratch += [pltpu.VMEM(shape, bf16), pltpu.SemaphoreType.DMA((NPEER,))]
    return pl.pallas_call(
        functools.partial(backward_kernel, which),
        out_shape=jax.ShapeDtypeStruct(shape, bf16) if which == 2 else pltpu.HBM(shape, bf16),
        in_specs=[smem(), hbm()] + [vmem()] * len(blocks),
        out_specs=vmem() if which == 2 else hbm(),
        scratch_shapes=scratch,
        compiler_params=params(),
        cost_estimate=TILES_COST,
        name="backward_tiles",
    )(in_hbm(lists), in_hbm(values), *blocks)


def dense_kernel(
    recv_ref, weight_ref, bias_ref, cot_ref, hidden_ref, grad_ref, wsum_ref, one, sems
):
    copies = []
    weight = weight_ref[...]
    for part in range(2):
        here = pl.ds(part * 2 * TILE, 2 * TILE)
        total = recv_ref[0, here, :].astype(f32)
        for peer in range(1, NPEER):
            total += recv_ref[peer, here, :].astype(f32)
        agg = total.astype(bf16)
        v = jnp.dot(agg, weight, preferred_element_type=f32) + bias_ref[...]
        s = jnp.tanh(gelu_coef * (v + cube_coef * v * v * v))
        hidden_ref[here, :] = (0.5 * v * (1.0 + s)).astype(bf16)
        slope = 0.5 * (1.0 + s) + 0.5 * v * (1.0 - s * s) * gelu_coef * (
            1.0 + 3.0 * cube_coef * v * v
        )
        grad = (cot_ref[here, :].astype(f32) * slope).astype(bf16)
        wsum = lax.dot_general(agg, grad, (((0,), (0,)), ((), ())), preferred_element_type=f32)
        bsum = jnp.dot(jnp.ones((16, 2 * TILE), bf16), grad, preferred_element_type=f32)[:8]
        back = lax.dot_general(weight, grad, (((1,), (1,)), ((), ())), preferred_element_type=f32)
        back = back.astype(bf16)
        for sub in range(2):
            rows = pl.ds((part * 2 + sub) * FEAT, FEAT)
            one[rows, :] = back[:, sub * TILE : (sub + 1) * TILE]
        rows = pl.ds(part * 2 * FEAT, 2 * FEAT)
        for peer in range(NPEER):
            copies.append(
                pltpu.make_async_copy(
                    one.at[rows], grad_ref.at[peer, rows], sems.at[part * NPEER + peer]
                )
            )
            copies[-1].start()
        if part == 0:
            wsum_ref[pl.ds(0, FEAT), :] = wsum
            wsum_ref[pl.ds(FEAT, 8), :] = bsum
        else:
            wsum_ref[pl.ds(0, FEAT), :] += wsum
            wsum_ref[pl.ds(FEAT, 8), :] += bsum
    for copy in copies:
        copy.wait()


def dense(recv, weight, bias, cotangent):
    return pl.pallas_call(
        dense_kernel,
        out_shape=(
            jax.ShapeDtypeStruct((4 * TILE, FEAT), bf16),
            pltpu.HBM((NPEER, 4 * FEAT, TILE), bf16),
            jax.ShapeDtypeStruct((FEAT + 8, FEAT), f32),
        ),
        in_specs=[vmem()] * 4,
        out_specs=(vmem(), hbm(), vmem()),
        scratch_shapes=[
            pltpu.VMEM((4 * FEAT, TILE), bf16),
            pltpu.SemaphoreType.DMA((2 * NPEER,)),
        ],
        compiler_params=params(),
        cost_estimate=pl.CostEstimate(
            flops=6 * 1024 * FEAT * FEAT, bytes_accessed=5 * 2**20, transcendentals=1024 * FEAT
        ),
        name="dense_layer",
    )(recv, weight, bias, cotangent)


def last_kernel(recv_ref, grad_ref):
    for sub in range(4):
        rows = pl.ds(sub * FEAT, FEAT)
        total = recv_ref[0, rows, :].astype(f32)
        for peer in range(1, NPEER):
            total += recv_ref[peer, rows, :].astype(f32)
        grad_ref[pl.ds(sub * TILE, TILE), :] = total.T.astype(bf16)


def last(recv):
    return pl.pallas_call(
        last_kernel,
        out_shape=jax.ShapeDtypeStruct((4 * TILE, FEAT), bf16),
        in_specs=[vmem()],
        out_specs=vmem(),
        compiler_params=params(),
        cost_estimate=pl.CostEstimate(flops=2**20, bytes_accessed=3 * 2**20, transcendentals=0),
        name="last_sum",
    )(recv)


SAME_CORE = [[2 * j + core for j in range(NPEER)] for core in range(2)]
OTHER_CORE = [(r, r ^ 1) for r in range(16)]


def to_other_core(value):
    return lax.ppermute(value, "row", OTHER_CORE)


def row_exchange(value):
    return lax.all_to_all(value, "row", 0, 0, axis_index_groups=SAME_CORE)


def col_exchange(value):
    return lax.all_to_all(value, "col", 0, 0)


def partner(value, axis, size, bit):
    return lax.ppermute(value, axis, [(i, i ^ bit) for i in range(size)])


def local(features, weight, layer_bias, cotangent, tile_out, tile_in, tile_vals, tile_count):
    values = tile_vals[0, 0]
    where = (lax.axis_index("row") & 1).astype(jnp.int32).reshape(1)
    lists = prep(where, tile_out[0, 0], tile_in[0, 0], tile_count[0])
    bias = layer_bias.reshape(1, FEAT)
    order = lax.optimization_barrier

    sources = col_exchange(copies_of(features))
    other = forward(1, lists, values, sources)
    other, lists = order((other, lists))
    mine = forward(0, lists, values, sources)
    recv = row_exchange(pair_sum(mine, to_other_core(other)))
    hidden, grad, total = dense(recv, weight, bias, cotangent)

    grads = row_exchange(grad)
    for bit in (2, 4):
        total = total + partner(total, "col", 8, bit)
    total = total + partner(total, "row", 16, 1)
    total = total + partner(total, "col", 8, 1)
    grads, total = order((grads, total))
    other = to_other_core(grads)
    second = partner(total, "row", 16, 2)
    back = backward(2, lists, values, grads)
    back = backward(3, lists, values, other, back)
    back, second = order((back, second))
    total = total + second
    back = col_exchange(back)
    for bit in (4, 8):
        total = total + partner(total, "row", 16, bit)
    scale = 1.0 / math.sqrt(4 * TILE * 128)
    weight_grad = total[:FEAT] * scale
    bias_grad = total[FEAT] * scale
    back, weight_grad, bias_grad = order((back, weight_grad, bias_grad))
    feature_grad = last(back)
    return (hidden, feature_grad, weight_grad, bias_grad)


def solution(mesh):
    in_specs = (
        P(("row", "col"), None),
        P(),
        P(),
        P(("col", "row"), None),
        P("row", "col", None),
        P("row", "col", None),
        P("row", "col", None, None, None),
        P("row", "col"),
    )
    out_specs = (P(("col", "row"), None), P(("row", "col"), None), P(), P())
    return jax.shard_map(local, mesh=mesh, in_specs=in_specs, out_specs=out_specs, check_vma=False)
```

profile of v0, /device:TPU:0, one launch (start us, length us, event | category | flops | bytes accessed | tf_op | source)
XLA Modules:
  0.0 227.6 jit_solution(16698627784820357385)
XLA Ops:
  0.6 64.7 %copies.1 = bf16[8,1024,128]{2,1,0:T(8,128)(2,1)} custom-call(bf16[1024,128]{1,0:T(8,128)(2,1)} %value_ref.1), custom_call_target="tpu_custom_call" | custom-call | tf_op jit(solution)/shard_map/copies/pallas_call | solution.py:93
  65.3 0.0 copy-start.3
  65.4 0.0 copy-start.4
  65.4 6.4 %all-to-all-start = ((bf16[8,1024,128]{2,1,0:T(8,128)(2,1)}), bf16[8,1024,128]{2,1,0:T(8,128)(2,1)S(1)}, u32[]{:S(2)}, u32[]{:S(2)}) async-start(bf16[8,1024,128]{2,1,0:T(8,128)(2,1)} %copies.1), calls=%async_computation | async-start | bytes 4194304 | tf_op jit(solution)/shard_map/all_to_all | solution.py:360
  72.4 0.0 copy-done.3
  72.4 0.0 copy-done.4
  72.5 2.7 %slot_lists.1.lists_ref = s32[1024]{0:T(1024)S(1)} custom-call(s32[1]{0:T(128)} %bitcast.where_ref, s32[128]{0:T(128)S(1)} %bitcast.9, s32[128]{0:T(128)S(1)} %bitcast.10, s32[1]{0:T(128)} %bitcast.8.count_ref), custom_call_target="tpu_custom_call" | custom-call | tf_op jit(solution)/shard_map/slot_lists/pallas_call | solution.py:72
  75.2 0.0 copy-start.1
  75.2 0.6 copy-done.1
  75.8 23.0 %all-to-all-done.x = bf16[8,1024,128]{2,1,0:T(8,128)(2,1)S(1)} async-done(((bf16[8,1024,128]{2,1,0:T(8,128)(2,1)}), bf16[8,1024,128]{2,1,0:T(8,128)(2,1)S(1)}, u32[]{:S(2)}, u32[]{:S(2)}) %all-to-all-start) | async-done | bytes 2097184 | tf_op jit(solution)/shard_map/all_to_all | solution.py:360
  98.8 3.4 %forward_tiles.2 = bf16[8,1024,128]{2,1,0:T(8,128)(2,1)S(1)} custom-call(s32[1024]{0:T(1024)} %copy-done.1, bf16[128,256,256]{2,1,0:T(8,128)(2,1)} %bitcast.12, bf16[8,1024,128]{2,1,0:T(8,128)(2,1)S(1)} %all-to-all-done.x), custom_call_target="tpu_custom_call" | custom-call | flops 1073741824 | bytes 16777216 | tf_op jit(solution)/shard_map/forward_tiles/pallas_call | solution.py:172
  102.2 0.1 collective-permute-start
  102.3 2.9 %forward_tiles.3.mine_ref = bf16[8,1024,128]{2,1,0:T(8,128)(2,1)S(1)} custom-call(s32[1024]{0:T(1024)} %copy-done.1, bf16[128,256,256]{2,1,0:T(8,128)(2,1)} %bitcast.13, bf16[8,1024,128]{2,1,0:T(8,128)(2,1)S(1)} %all-to-all-done.x), custom_call_target="tpu_custom_call" | custom-call | flops 1073741824 | bytes 16777216 | tf_op jit(solution)/shard_map/forward_tiles/pallas_call | solution.py:172
  105.2 1.2 collective-permute-done.other_ref
  106.4 0.5 pair_sum.1
  106.9 0.0 copy-start
  106.9 0.0 copy-start.2
  106.9 0.0 copy-start.5
  106.9 39.8 %all_to_all.20.recv_ref = bf16[8,1024,128]{2,1,0:T(8,128)(2,1)S(1)} all-to-all(bf16[8,1024,128]{2,1,0:T(8,128)(2,1)S(1)} %pair_sum.1), channel_id=1, replica_groups={{0,16,32,48,64,80,96,112},{8,24,40,56,72,88,104,120},{1,17,33,49,65,81,..., dimensions={0} | all-to-all | bytes 4194304 | tf_op jit(solution)/shard_map/all_to_all | solution.py:356
  146.7 0.0 copy-done
  146.7 0.0 copy-done.2
  146.7 0.0 copy-done.5
  146.7 2.9 %dense_layer.1 = (bf16[1024,128]{1,0:T(8,128)(2,1)}, bf16[8,512,256]{2,1,0:T(8,128)(2,1)}, f32[136,128]{1,0:T(8,128)S(1)}) custom-call(bf16[8,1024,128]{2,1,0:T(8,128)(2,1)S(1)} %all_to_all.20.recv_ref, bf16[128,128]{1,0:T(8,128)(2,1)S(1)} %copy-done.2, f32[1,128]{1,0:T(1,128)S(1)} %bitcast.11, bf16[1024,128]{1,0:T(8,128)(2,1)S(1)} %copy-done), custom_call_target="tpu_custom_call" | custom-call | flops 100663296 | bytes 5242880 | tf_op jit(solution)/shard_map/dense_layer/pallas_call | solution.py:305
  149.7 3.6 %all-to-all-start.2 = ((bf16[8,512,256]{2,1,0:T(8,128)(2,1)}), bf16[8,512,256]{2,1,0:T(8,128)(2,1)S(1)}, u32[]{:S(2)}, u32[]{:S(2)}) async-start(bf16[8,512,256]{2,1,0:T(8,128)(2,1)} %get-tuple-element.19), calls=%async_computation.2 | async-start | bytes 4194304 | tf_op jit(solution)/shard_map/all_to_all | solution.py:356
  153.3 0.1 collective-permute-start.1
  153.4 4.3 %collective-permute-done.1 = f32[136,128]{1,0:T(8,128)S(1)} collective-permute-done((f32[136,128]{1,0:T(8,128)S(1)}, f32[136,128]{1,0:T(8,128)S(1)}, u32[]{:S(2)}, u32[]{:S(2)}) %collective-permute-start.1) | collective-permute-done | bytes 69664 | tf_op jit(solution)/shard_map/ppermute | solution.py:364
  157.7 0.9 collective-permute-start.2
  158.6 5.0 %collective-permute-done.2 = f32[136,128]{1,0:T(8,128)S(1)} collective-permute-done((f32[136,128]{1,0:T(8,128)S(1)}, f32[136,128]{1,0:T(8,128)S(1)}, u32[]{:S(2)}, u32[]{:S(2)}) %collective-permute-start.2) | collective-permute-done | bytes 69664 | tf_op jit(solution)/shard_map/ppermute | solution.py:364
  163.6 0.1 collective-permute-start.3
  163.7 1.2 collective-permute-done.3
  165.0 0.1 collective-permute-start.4
  165.1 7.4 %collective-permute-done.4 = f32[136,128]{1,0:T(8,128)S(1)} collective-permute-done((f32[136,128]{1,0:T(8,128)S(1)}, f32[136,128]{1,0:T(8,128)S(1)}, u32[]{:S(2)}, u32[]{:S(2)}) %collective-permute-start.4) | collective-permute-done | bytes 69664 | tf_op jit(solution)/shard_map/ppermute | solution.py:364
  172.5 12.1 %all-to-all-done.2.g = bf16[8,512,256]{2,1,0:T(8,128)(2,1)S(1)} async-done(((bf16[8,512,256]{2,1,0:T(8,128)(2,1)}), bf16[8,512,256]{2,1,0:T(8,128)(2,1)S(1)}, u32[]{:S(2)}, u32[]{:S(2)}) %all-to-all-start.2) | async-done | bytes 2097184 | tf_op jit(solution)/shard_map/all_to_all | solution.py:356
  184.6 0.0 collective-permute-start.5
  184.6 1.7 collective-permute-start.6
  186.2 2.8 %backward_tiles.2.rest_0_ = bf16[8,512,256]{2,1,0:T(8,128)(2,1)S(1)} custom-call(s32[1024]{0:T(1024)} %copy-done.1, bf16[128,256,256]{2,1,0:T(8,128)(2,1)} %bitcast.14, bf16[8,512,256]{2,1,0:T(8,128)(2,1)S(1)} %all-to-all-done.2.g), custom_call_target="tpu_custom_call" | custom-call | flops 1073741824 | bytes 16777216 | tf_op jit(solution)/shard_map/backward_tiles/pallas_call | solution.py:249
  189.1 0.0 collective-permute-done.5.g
  189.1 4.4 %backward_tiles.3 = bf16[8,512,256]{2,1,0:T(8,128)(2,1)} custom-call(s32[1024]{0:T(1024)} %copy-done.1, bf16[128,256,256]{2,1,0:T(8,128)(2,1)} %bitcast.15, bf16[8,512,256]{2,1,0:T(8,128)(2,1)S(1)} %collective-permute-done.5.g, bf16[8,512,256]{2,1,0:T(8,128)(2,1)S(1)} %backward_tiles.2.rest_0_), custom_call_target="tpu_custom_call" | custom-call | flops 1073741824 | bytes 16777216 | tf_op jit(solution)/shard_map/backward_tiles/pallas_call | solution.py:249
  193.5 0.0 collective-permute-done.6
  193.5 7.9 %all-to-all-start.3 = ((bf16[8,512,256]{2,1,0:T(8,128)(2,1)}), bf16[8,512,256]{2,1,0:T(8,128)(2,1)S(1)}, u32[]{:S(2)}, u32[]{:S(2)}) async-start(bf16[8,512,256]{2,1,0:T(8,128)(2,1)} %backward_tiles.3), calls=%async_computation.3 | async-start | bytes 4194304 | tf_op jit(solution)/shard_map/all_to_all | solution.py:360
  201.4 0.1 collective-permute-start.7
  201.5 4.3 %collective-permute-done.7 = f32[136,128]{1,0:T(8,128)S(1)} collective-permute-done((f32[136,128]{1,0:T(8,128)S(1)}, f32[136,128]{1,0:T(8,128)S(1)}, u32[]{:S(2)}, u32[]{:S(2)}) %collective-permute-start.7) | collective-permute-done | bytes 69664 | tf_op jit(solution)/shard_map/ppermute | solution.py:364
  205.8 0.4 collective-permute-start.8
  206.1 5.5 %collective-permute-done.8 = f32[136,128]{1,0:T(8,128)S(1)} collective-permute-done((f32[136,128]{1,0:T(8,128)S(1)}, f32[136,128]{1,0:T(8,128)S(1)}, u32[]{:S(2)}, u32[]{:S(2)}) %collective-permute-start.8) | collective-permute-done | bytes 69664 | tf_op jit(solution)/shard_map/ppermute | solution.py:364
  211.7 0.5 fusion
  212.2 0.6 slice_multiply_fusion
  212.8 13.7 %all-to-all-done.3.recv_ref = bf16[8,512,256]{2,1,0:T(8,128)(2,1)S(1)} async-done(((bf16[8,512,256]{2,1,0:T(8,128)(2,1)}), bf16[8,512,256]{2,1,0:T(8,128)(2,1)S(1)}, u32[]{:S(2)}, u32[]{:S(2)}) %all-to-all-start.3) | async-done | bytes 2097184 | tf_op jit(solution)/shard_map/all_to_all | solution.py:360
  226.5 1.0 last_sum.1
  (7 shorter events, 0.1 us)
Async XLA Ops:
  65.3 7.1 %copy-start.3 = (s32[1,1,128]{2,1,0:T(1,128)S(1)}, s32[1,1,128]{2,1,0:T(1,128)}, u32[]{:S(2)}) copy-start(s32[1,1,128]{2,1,0:T(1,128)} %param.12) | copy-start | bytes 1540
  65.4 7.1 %copy-start.4 = (s32[1,1,128]{2,1,0:T(1,128)S(1)}, s32[1,1,128]{2,1,0:T(1,128)}, u32[]{:S(2)}) copy-start(s32[1,1,128]{2,1,0:T(1,128)} %param.13) | copy-start | bytes 1540
  65.4 33.4 %all-to-all-start = ((bf16[8,1024,128]{2,1,0:T(8,128)(2,1)}), bf16[8,1024,128]{2,1,0:T(8,128)(2,1)S(1)}, u32[]{:S(2)}, u32[]{:S(2)}) async-start(bf16[8,1024,128]{2,1,0:T(8,128)(2,1)} %copies.1), calls=%async_computation | async-start | bytes 4194304 | tf_op jit(solution)/shard_map/all_to_all | solution.py:360
  75.2 0.6 copy-start.1
  102.2 4.2 %collective-permute-start = (bf16[8,1024,128]{2,1,0:T(8,128)(2,1)S(1)}, bf16[8,1024,128]{2,1,0:T(8,128)(2,1)S(1)}, u32[]{:S(2)}, u32[]{:S(2)}) collective-permute-start(bf16[8,1024,128]{2,1,0:T(8,128)(2,1)S(1)} %forward_tiles.2), channel_id=1, source_target_pairs={{0,8},{8,0},{16,24},{24,16},{32,40},{40,32},{48,56},{56,48},{64,72... | collective-permute-start | bytes 6291464 | tf_op jit(solution)/shard_map/ppermute | solution.py:352
  106.9 39.9 %copy-start = (bf16[1024,128]{1,0:T(8,128)(2,1)S(1)}, bf16[1024,128]{1,0:T(8,128)(2,1)}, u32[]{:S(2)}) copy-start(bf16[1024,128]{1,0:T(8,128)(2,1)} %cot_ref.1) | copy-start | bytes 786436
  106.9 39.8 %copy-start.2 = (bf16[128,128]{1,0:T(8,128)(2,1)S(1)}, bf16[128,128]{1,0:T(8,128)(2,1)}, u32[]{:S(2)}) copy-start(bf16[128,128]{1,0:T(8,128)(2,1)} %weight_ref.1) | copy-start | bytes 98308
  106.9 39.8 %copy-start.5 = (f32[128]{0:T(128)S(1)}, f32[128]{0:T(128)}, u32[]{:S(2)}) copy-start(f32[128]{0:T(128)} %param.10) | copy-start | bytes 1540
  149.7 34.9 %all-to-all-start.2 = ((bf16[8,512,256]{2,1,0:T(8,128)(2,1)}), bf16[8,512,256]{2,1,0:T(8,128)(2,1)S(1)}, u32[]{:S(2)}, u32[]{:S(2)}) async-start(bf16[8,512,256]{2,1,0:T(8,128)(2,1)} %get-tuple-element.19), calls=%async_computation.2 | async-start | bytes 4194304 | tf_op jit(solution)/shard_map/all_to_all | solution.py:356
  153.3 4.4 %collective-permute-start.1 = (f32[136,128]{1,0:T(8,128)S(1)}, f32[136,128]{1,0:T(8,128)S(1)}, u32[]{:S(2)}, u32[]{:S(2)}) collective-permute-start(f32[136,128]{1,0:T(8,128)S(1)} %get-tuple-element.20), channel_id=1, source_target_pairs={{0,2},{1,3},{2,0},{3,1},{4,6},{5,7},{6,4},{7,5},{8,10},{9,11},{10,... | collective-permute-start | bytes 208904 | tf_op jit(solution)/shard_map/ppermute | solution.py:364
  157.7 5.9 %collective-permute-start.2 = (f32[136,128]{1,0:T(8,128)S(1)}, f32[136,128]{1,0:T(8,128)S(1)}, u32[]{:S(2)}, u32[]{:S(2)}) collective-permute-start(f32[136,128]{1,0:T(8,128)S(1)} %add.21), channel_id=1, source_target_pairs={{0,4},{1,5},{2,6},{3,7},{4,0},{5,1},{6,2},{7,3},{8,12},{9,13},{10,... | collective-permute-start | bytes 208904 | tf_op jit(solution)/shard_map/ppermute | solution.py:364
  163.6 1.3 collective-permute-start.3
  165.0 7.5 %collective-permute-start.4 = (f32[136,128]{1,0:T(8,128)S(1)}, f32[136,128]{1,0:T(8,128)S(1)}, u32[]{:S(2)}, u32[]{:S(2)}) collective-permute-start(f32[136,128]{1,0:T(8,128)S(1)} %add.23), channel_id=1, source_target_pairs={{0,1},{1,0},{2,3},{3,2},{4,5},{5,4},{6,7},{7,6},{8,9},{9,8},{10,11... | collective-permute-start | bytes 208904 | tf_op jit(solution)/shard_map/ppermute | solution.py:364
  184.6 4.5 %collective-permute-start.5 = (bf16[8,512,256]{2,1,0:T(8,128)(2,1)S(1)}, bf16[8,512,256]{2,1,0:T(8,128)(2,1)S(1)}, u32[]{:S(2)}, u32[]{:S(2)}) collective-permute-start(bf16[8,512,256]{2,1,0:T(8,128)(2,1)S(1)} %all-to-all-done.2.g), channel_id=1, source_target_pairs={{0,8},{8,0},{16,24},{24,16},{32,40},{40,32},{48,56},{56,48},{64,72... | collective-permute-start | bytes 6291464 | tf_op jit(solution)/shard_map/ppermute | solution.py:352
  184.6 8.9 %collective-permute-start.6 = (f32[136,128]{1,0:T(8,128)S(1)}, f32[136,128]{1,0:T(8,128)S(1)}, u32[]{:S(2)}, u32[]{:S(2)}) collective-permute-start(f32[136,128]{1,0:T(8,128)S(1)} %add.24), channel_id=1, source_target_pairs={{0,16},{8,24},{16,0},{24,8},{32,48},{40,56},{48,32},{56,40},{64,80... | collective-permute-start | bytes 208904 | tf_op jit(solution)/shard_map/ppermute | solution.py:364
  193.5 33.0 %all-to-all-start.3 = ((bf16[8,512,256]{2,1,0:T(8,128)(2,1)}), bf16[8,512,256]{2,1,0:T(8,128)(2,1)S(1)}, u32[]{:S(2)}, u32[]{:S(2)}) async-start(bf16[8,512,256]{2,1,0:T(8,128)(2,1)} %backward_tiles.3), calls=%async_computation.3 | async-start | bytes 4194304 | tf_op jit(solution)/shard_map/all_to_all | solution.py:360
  201.4 4.4 %collective-permute-start.7 = (f32[136,128]{1,0:T(8,128)S(1)}, f32[136,128]{1,0:T(8,128)S(1)}, u32[]{:S(2)}, u32[]{:S(2)}) collective-permute-start(f32[136,128]{1,0:T(8,128)S(1)} %add.25), channel_id=1, source_target_pairs={{0,32},{8,40},{16,48},{24,56},{32,0},{40,8},{48,16},{56,24},{64,96... | collective-permute-start | bytes 208904 | tf_op jit(solution)/shard_map/ppermute | solution.py:364
  205.8 5.9 %collective-permute-start.8 = (f32[136,128]{1,0:T(8,128)S(1)}, f32[136,128]{1,0:T(8,128)S(1)}, u32[]{:S(2)}, u32[]{:S(2)}) collective-permute-start(f32[136,128]{1,0:T(8,128)S(1)} %add.26), channel_id=1, source_target_pairs={{0,64},{8,72},{16,80},{24,88},{32,96},{40,104},{48,112},{56,120},{... | collective-permute-start | bytes 208904 | tf_op jit(solution)/shard_map/ppermute | solution.py:364
where the time goes:
time: 228 us
  Pallas kernels  85.4 us (37%)
  waiting for transfers between devices  77.7 us (34%)
  blocking collectives  39.8 us (17%)
  starting transfers between devices  21.3 us (9%)
    pallas_call x1, Pallas kernels, copies_of(): pl.pallas_call(copies_kernel, out_shape=pltpu.HBM((NPEER, *value.shape),...  64.7 us
    all_to_all x1, blocking collectives, row_exchange(): return lax.all_to_all(value, 'row', 0, 0, axis_index_groups=SAME_CORE)  39.8 us
    all_to_all x2, waiting for transfers between devices, col_exchange(): return lax.all_to_all(value, 'col', 0, 0)  36.7 us
    ppermute x7, waiting for transfers between devices, partner(): return lax.ppermute(value, axis, [(i, i ^ bit) for i in range(size)])  27.8 us
    all_to_all x2, starting transfers between devices, col_exchange(): return lax.all_to_all(value, 'col', 0, 0)  14.3 us
    all_to_all x1, waiting for transfers between devices, row_exchange(): return lax.all_to_all(value, 'row', 0, 0, axis_index_groups=SAME_CORE)  12.1 us
    pallas_call x2, Pallas kernels, backward(): pl.pallas_call(functools.partial(backward_kernel, which), out_shape=jax.S...  7.23 us
    pallas_call x2, Pallas kernels, forward(): pl.pallas_call(functools.partial(forward_kernel, which), out_shape=jax.Sh...  6.34 us
  transfers between devices with their start and end apart: 12, of which 10 were waited for; matrix products, arithmetic and copies ran while one was open for 1% of the time, Pallas kernels for 6%

commit v1 on v0

--- a/solution.py
+++ b/solution.py
@@ -79,10 +79,11 @@
     )(where, out_index, in_index, count)
 
 
-def copies_kernel(value_ref, out_ref, sems):
-    copies = [
-        pltpu.make_async_copy(value_ref, out_ref.at[peer], sems.at[peer]) for peer in range(NPEER)
-    ]
+def copies_kernel(value_ref, out_ref, held, in_sem, sems):
+    fetch = pltpu.make_async_copy(value_ref, held, in_sem)
+    fetch.start()
+    fetch.wait()
+    copies = [pltpu.make_async_copy(held, out_ref.at[peer], sems.at[peer]) for peer in range(NPEER)]
     for copy in copies:
         copy.start()
     for copy in copies:
@@ -95,7 +96,11 @@
         out_shape=pltpu.HBM((NPEER, *value.shape), value.dtype),
         in_specs=[hbm()],
         out_specs=hbm(),
-        scratch_shapes=[pltpu.SemaphoreType.DMA((NPEER,))],
+        scratch_shapes=[
+            pltpu.VMEM(value.shape, value.dtype),
+            pltpu.SemaphoreType.DMA,
+            pltpu.SemaphoreType.DMA((NPEER,)),
+        ],
         compiler_params=params(),
         name="copies",
     )(in_hbm(value))
@@ -263,8 +268,8 @@
 ):
     copies = []
     weight = weight_ref[...]
-    for part in range(2):
-        here = pl.ds(part * 2 * TILE, 2 * TILE)
+    for part in range(4):
+        here = pl.ds(part * TILE, TILE)
         total = recv_ref[0, here, :].astype(f32)
         for peer in range(1, NPEER):
             total += recv_ref[peer, here, :].astype(f32)
@@ -277,13 +282,11 @@
         )
         grad = (cot_ref[here, :].astype(f32) * slope).astype(bf16)
         wsum = lax.dot_general(agg, grad, (((0,), (0,)), ((), ())), preferred_element_type=f32)
-        bsum = jnp.dot(jnp.ones((16, 2 * TILE), bf16), grad, preferred_element_type=f32)[:8]
+        bsum = jnp.dot(jnp.ones((16, TILE), bf16), grad, preferred_element_type=f32)[:8]
         back = lax.dot_general(weight, grad, (((1,), (1,)), ((), ())), preferred_element_type=f32)
         back = back.astype(bf16)
-        for sub in range(2):
-            rows = pl.ds((part * 2 + sub) * FEAT, FEAT)
-            one[rows, :] = back[:, sub * TILE : (sub + 1) * TILE]
-        rows = pl.ds(part * 2 * FEAT, 2 * FEAT)
+        rows = pl.ds(part * FEAT, FEAT)
+        one[rows, :] = back
         for peer in range(NPEER):
             copies.append(
                 pltpu.make_async_copy(
@@ -313,7 +316,7 @@
         out_specs=(vmem(), hbm(), vmem()),
         scratch_shapes=[
             pltpu.VMEM((4 * FEAT, TILE), bf16),
-            pltpu.SemaphoreType.DMA((2 * NPEER,)),
+            pltpu.SemaphoreType.DMA((4 * NPEER,)),
         ],
         compiler_params=params(),
         cost_estimate=pl.CostEstimate(

time: 228 us -> 165 us (0.72)
  Pallas kernels: 85.4 us -> 23.6 us
  starting transfers between devices: 21.3 us -> 29.8 us
  waiting for transfers between devices: 77.7 us -> 69.7 us
  blocking collectives: 39.8 us -> 36.1 us
    pallas_call x1, Pallas kernels: 64.7 us -> 2.36 us  [copies_of(): pl.pallas_call(copies_kernel, out_shape=pltpu.HBM((NPEER, *value.shape),...]
    ppermute x7, starting transfers between devices: 3.28 us -> 15.8 us  [partner(): return lax.ppermute(value, axis, [(i, i ^ bit) for i in range(size)])]
    ppermute x7, waiting for transfers between devices: 27.8 us -> 21.6 us  [partner(): return lax.ppermute(value, axis, [(i, i ^ bit) for i in range(size)])]
    all_to_all x2, starting transfers between devices: 14.3 us -> 10 us  [col_exchange(): return lax.all_to_all(value, 'col', 0, 0)]
    all_to_all x1, blocking collectives: 39.8 us -> 36.1 us  [row_exchange(): return lax.all_to_all(value, 'row', 0, 0, axis_index_groups=SAME_CORE)]
    all_to_all x1, waiting for transfers between devices: 12.1 us -> 9.5 us  [row_exchange(): return lax.all_to_all(value, 'row', 0, 0, axis_index_groups=SAME_CORE)]
  transfers between devices with their start and end apart: 12 -> 12, of which waited for: 10 -> 10; matrix products, arithmetic and copies ran while one was open for 1% -> 1% of each run, Pallas kernels for 6% -> 8%
where the time goes in v1:
time: 165 us; the launch traced here: 162 us
  waiting for transfers between devices  69.7 us (42%)
  blocking collectives  36.1 us (22%)
  starting transfers between devices  29.8 us (18%)
  Pallas kernels  23.6 us (14%)
    all_to_all x2, waiting for transfers between devices, col_exchange(): return lax.all_to_all(value, 'col', 0, 0)  38 us
    all_to_all x1, blocking collectives, row_exchange(): return lax.all_to_all(value, 'row', 0, 0, axis_index_groups=SAME_CORE)  36.1 us
    ppermute x7, waiting for transfers between devices, partner(): return lax.ppermute(value, axis, [(i, i ^ bit) for i in range(size)])  21.6 us
    ppermute x7, starting transfers between devices, partner(): return lax.ppermute(value, axis, [(i, i ^ bit) for i in range(size)])  15.8 us
    all_to_all x2, starting transfers between devices, col_exchange(): return lax.all_to_all(value, 'col', 0, 0)  10 us
    all_to_all x1, waiting for transfers between devices, row_exchange(): return lax.all_to_all(value, 'row', 0, 0, axis_index_groups=SAME_CORE)  9.5 us
    pallas_call x2, Pallas kernels, backward(): pl.pallas_call(functools.partial(backward_kernel, which), out_shape=jax.S...  7.48 us
    pallas_call x2, Pallas kernels, forward(): pl.pallas_call(functools.partial(forward_kernel, which), out_shape=jax.Sh...  6.49 us
  transfers between devices with their start and end apart: 12, of which 10 were waited for; matrix products, arithmetic and copies ran while one was open for 1% of the time, Pallas kernels for 8%

profile of v1, /device:TPU:0, one launch (start us, length us, event | category | flops | bytes accessed | tf_op | source)
XLA Modules:
  0.0 162.5 jit_solution(11465482221501305411)
XLA Ops:
  0.6 2.4 %copies.1 = bf16[8,1024,128]{2,1,0:T(8,128)(2,1)} custom-call(bf16[1024,128]{1,0:T(8,128)(2,1)} %value_ref.1), custom_call_target="tpu_custom_call" | custom-call | tf_op jit(solution)/shard_map/copies/pallas_call | solution.py:94
  3.0 0.0 copy-start.3
  3.0 0.0 copy-start.4
  3.0 6.4 %all-to-all-start = ((bf16[8,1024,128]{2,1,0:T(8,128)(2,1)}), bf16[8,1024,128]{2,1,0:T(8,128)(2,1)S(1)}, u32[]{:S(2)}, u32[]{:S(2)}) async-start(bf16[8,1024,128]{2,1,0:T(8,128)(2,1)} %copies.1), calls=%async_computation | async-start | bytes 4194304 | tf_op jit(solution)/shard_map/all_to_all | solution.py:363
  10.1 0.0 copy-done.3
  10.1 0.0 copy-done.4
  10.1 2.7 %slot_lists.1.lists_ref = s32[1024]{0:T(1024)S(1)} custom-call(s32[1]{0:T(128)} %bitcast.where_ref, s32[128]{0:T(128)S(1)} %bitcast.9, s32[128]{0:T(128)S(1)} %bitcast.10, s32[1]{0:T(128)} %bitcast.8.count_ref), custom_call_target="tpu_custom_call" | custom-call | tf_op jit(solution)/shard_map/slot_lists/pallas_call | solution.py:72
  12.8 0.0 copy-start.1
  12.8 0.6 copy-done.1
  13.4 23.0 %all-to-all-done.x = bf16[8,1024,128]{2,1,0:T(8,128)(2,1)S(1)} async-done(((bf16[8,1024,128]{2,1,0:T(8,128)(2,1)}), bf16[8,1024,128]{2,1,0:T(8,128)(2,1)S(1)}, u32[]{:S(2)}, u32[]{:S(2)}) %all-to-all-start) | async-done | bytes 2097184 | tf_op jit(solution)/shard_map/all_to_all | solution.py:363
  36.4 2.9 %forward_tiles.2 = bf16[8,1024,128]{2,1,0:T(8,128)(2,1)S(1)} custom-call(s32[1024]{0:T(1024)} %copy-done.1, bf16[128,256,256]{2,1,0:T(8,128)(2,1)} %bitcast.12, bf16[8,1024,128]{2,1,0:T(8,128)(2,1)S(1)} %all-to-all-done.x), custom_call_target="tpu_custom_call" | custom-call | flops 1073741824 | bytes 16777216 | tf_op jit(solution)/shard_map/forward_tiles/pallas_call | solution.py:177
  39.4 0.1 collective-permute-start
  39.5 3.5 %forward_tiles.3.mine_ref = bf16[8,1024,128]{2,1,0:T(8,128)(2,1)S(1)} custom-call(s32[1024]{0:T(1024)} %copy-done.1, bf16[128,256,256]{2,1,0:T(8,128)(2,1)} %bitcast.13, bf16[8,1024,128]{2,1,0:T(8,128)(2,1)S(1)} %all-to-all-done.x), custom_call_target="tpu_custom_call" | custom-call | flops 1073741824 | bytes 16777216 | tf_op jit(solution)/shard_map/forward_tiles/pallas_call | solution.py:177
  43.0 0.6 collective-permute-done.other_ref
  43.6 0.5 pair_sum.1
  44.1 0.0 copy-start
  44.1 0.0 copy-start.2
  44.1 0.0 copy-start.5
  44.1 36.1 %all_to_all.20.recv_ref = bf16[8,1024,128]{2,1,0:T(8,128)(2,1)S(1)} all-to-all(bf16[8,1024,128]{2,1,0:T(8,128)(2,1)S(1)} %pair_sum.1), channel_id=1, replica_groups={{0,16,32,48,64,80,96,112},{8,24,40,56,72,88,104,120},{1,17,33,49,65,81,..., dimensions={0} | all-to-all | bytes 4194304 | tf_op jit(solution)/shard_map/all_to_all | solution.py:359
  80.2 0.0 copy-done
  80.2 0.0 copy-done.2
  80.2 0.0 copy-done.5
  80.2 3.0 %dense_layer.1 = (bf16[1024,128]{1,0:T(8,128)(2,1)}, bf16[8,512,256]{2,1,0:T(8,128)(2,1)}, f32[136,128]{1,0:T(8,128)S(1)}) custom-call(bf16[8,1024,128]{2,1,0:T(8,128)(2,1)S(1)} %all_to_all.20.recv_ref, bf16[128,128]{1,0:T(8,128)(2,1)S(1)} %copy-done.2, f32[1,128]{1,0:T(1,128)S(1)} %bitcast.11, bf16[1024,128]{1,0:T(8,128)(2,1)S(1)} %copy-done), custom_call_target="tpu_custom_call" | custom-call | flops 100663296 | bytes 5242880 | tf_op jit(solution)/shard_map/dense_layer/pallas_call | solution.py:308
  83.2 3.7 %all-to-all-start.2 = ((bf16[8,512,256]{2,1,0:T(8,128)(2,1)}), bf16[8,512,256]{2,1,0:T(8,128)(2,1)S(1)}, u32[]{:S(2)}, u32[]{:S(2)}) async-start(bf16[8,512,256]{2,1,0:T(8,128)(2,1)} %get-tuple-element.19), calls=%async_computation.2 | async-start | bytes 4194304 | tf_op jit(solution)/shard_map/all_to_all | solution.py:359
  87.0 1.9 %collective-permute-start.1 = (f32[136,128]{1,0:T(8,128)S(1)}, f32[136,128]{1,0:T(8,128)S(1)}, u32[]{:S(2)}, u32[]{:S(2)}) collective-permute-start(f32[136,128]{1,0:T(8,128)S(1)} %get-tuple-element.20), channel_id=1, source_target_pairs={{0,2},{1,3},{2,0},{3,1},{4,6},{5,7},{6,4},{7,5},{8,10},{9,11},{10,... | collective-permute-start | bytes 208904 | tf_op jit(solution)/shard_map/ppermute | solution.py:367
  88.9 2.8 %collective-permute-done.1 = f32[136,128]{1,0:T(8,128)S(1)} collective-permute-done((f32[136,128]{1,0:T(8,128)S(1)}, f32[136,128]{1,0:T(8,128)S(1)}, u32[]{:S(2)}, u32[]{:S(2)}) %collective-permute-start.1) | collective-permute-done | bytes 69664 | tf_op jit(solution)/shard_map/ppermute | solution.py:367
  91.7 2.5 %collective-permute-start.2 = (f32[136,128]{1,0:T(8,128)S(1)}, f32[136,128]{1,0:T(8,128)S(1)}, u32[]{:S(2)}, u32[]{:S(2)}) collective-permute-start(f32[136,128]{1,0:T(8,128)S(1)} %add.21), channel_id=1, source_target_pairs={{0,4},{1,5},{2,6},{3,7},{4,0},{5,1},{6,2},{7,3},{8,12},{9,13},{10,... | collective-permute-start | bytes 208904 | tf_op jit(solution)/shard_map/ppermute | solution.py:367
  94.3 3.4 %collective-permute-done.2 = f32[136,128]{1,0:T(8,128)S(1)} collective-permute-done((f32[136,128]{1,0:T(8,128)S(1)}, f32[136,128]{1,0:T(8,128)S(1)}, u32[]{:S(2)}, u32[]{:S(2)}) %collective-permute-start.2) | collective-permute-done | bytes 69664 | tf_op jit(solution)/shard_map/ppermute | solution.py:367
  97.6 0.1 collective-permute-start.3
  97.7 1.2 collective-permute-done.3
  99.0 2.1 %collective-permute-start.4 = (f32[136,128]{1,0:T(8,128)S(1)}, f32[136,128]{1,0:T(8,128)S(1)}, u32[]{:S(2)}, u32[]{:S(2)}) collective-permute-start(f32[136,128]{1,0:T(8,128)S(1)} %add.23), channel_id=1, source_target_pairs={{0,1},{1,0},{2,3},{3,2},{4,5},{5,4},{6,7},{7,6},{8,9},{9,8},{10,11... | collective-permute-start | bytes 208904 | tf_op jit(solution)/shard_map/ppermute | solution.py:367
  101.1 8.6 %collective-permute-done.4 = f32[136,128]{1,0:T(8,128)S(1)} collective-permute-done((f32[136,128]{1,0:T(8,128)S(1)}, f32[136,128]{1,0:T(8,128)S(1)}, u32[]{:S(2)}, u32[]{:S(2)}) %collective-permute-start.4) | collective-permute-done | bytes 69664 | tf_op jit(solution)/shard_map/ppermute | solution.py:367
  109.8 9.5 %all-to-all-done.2.g = bf16[8,512,256]{2,1,0:T(8,128)(2,1)S(1)} async-done(((bf16[8,512,256]{2,1,0:T(8,128)(2,1)}), bf16[8,512,256]{2,1,0:T(8,128)(2,1)S(1)}, u32[]{:S(2)}, u32[]{:S(2)}) %all-to-all-start.2) | async-done | bytes 2097184 | tf_op jit(solution)/shard_map/all_to_all | solution.py:359
  119.3 0.1 collective-permute-start.5
  119.4 3.5 %collective-permute-start.6 = (f32[136,128]{1,0:T(8,128)S(1)}, f32[136,128]{1,0:T(8,128)S(1)}, u32[]{:S(2)}, u32[]{:S(2)}) collective-permute-start(f32[136,128]{1,0:T(8,128)S(1)} %add.24), channel_id=1, source_target_pairs={{0,16},{8,24},{16,0},{24,8},{32,48},{40,56},{48,32},{56,40},{64,80... | collective-permute-start | bytes 208904 | tf_op jit(solution)/shard_map/ppermute | solution.py:367
  122.8 3.4 %backward_tiles.2.rest_0_ = bf16[8,512,256]{2,1,0:T(8,128)(2,1)S(1)} custom-call(s32[1024]{0:T(1024)} %copy-done.1, bf16[128,256,256]{2,1,0:T(8,128)(2,1)} %bitcast.14, bf16[8,512,256]{2,1,0:T(8,128)(2,1)S(1)} %all-to-all-done.2.g), custom_call_target="tpu_custom_call" | custom-call | flops 1073741824 | bytes 16777216 | tf_op jit(solution)/shard_map/backward_tiles/pallas_call | solution.py:254
  126.3 0.0 collective-permute-done.5.g
  126.3 4.1 %backward_tiles.3 = bf16[8,512,256]{2,1,0:T(8,128)(2,1)} custom-call(s32[1024]{0:T(1024)} %copy-done.1, bf16[128,256,256]{2,1,0:T(8,128)(2,1)} %bitcast.15, bf16[8,512,256]{2,1,0:T(8,128)(2,1)S(1)} %collective-permute-done.5.g, bf16[8,512,256]{2,1,0:T(8,128)(2,1)S(1)} %backward_tiles.2.rest_0_), custom_call_target="tpu_custom_call" | custom-call | flops 1073741824 | bytes 16777216 | tf_op jit(solution)/shard_map/backward_tiles/pallas_call | solution.py:254
  130.4 0.0 collective-permute-done.6
  130.4 3.6 %all-to-all-start.3 = ((bf16[8,512,256]{2,1,0:T(8,128)(2,1)}), bf16[8,512,256]{2,1,0:T(8,128)(2,1)S(1)}, u32[]{:S(2)}, u32[]{:S(2)}) async-start(bf16[8,512,256]{2,1,0:T(8,128)(2,1)} %backward_tiles.3), calls=%async_computation.3 | async-start | bytes 4194304 | tf_op jit(solution)/shard_map/all_to_all | solution.py:363
  134.0 3.1 %collective-permute-start.7 = (f32[136,128]{1,0:T(8,128)S(1)}, f32[136,128]{1,0:T(8,128)S(1)}, u32[]{:S(2)}, u32[]{:S(2)}) collective-permute-start(f32[136,128]{1,0:T(8,128)S(1)} %add.25), channel_id=1, source_target_pairs={{0,32},{8,40},{16,48},{24,56},{32,0},{40,8},{48,16},{56,24},{64,96... | collective-permute-start | bytes 208904 | tf_op jit(solution)/shard_map/ppermute | solution.py:367
  137.1 2.3 %collective-permute-done.7 = f32[136,128]{1,0:T(8,128)S(1)} collective-permute-done((f32[136,128]{1,0:T(8,128)S(1)}, f32[136,128]{1,0:T(8,128)S(1)}, u32[]{:S(2)}, u32[]{:S(2)}) %collective-permute-start.7) | collective-permute-done | bytes 69664 | tf_op jit(solution)/shard_map/ppermute | solution.py:367
  139.4 2.6 %collective-permute-start.8 = (f32[136,128]{1,0:T(8,128)S(1)}, f32[136,128]{1,0:T(8,128)S(1)}, u32[]{:S(2)}, u32[]{:S(2)}) collective-permute-start(f32[136,128]{1,0:T(8,128)S(1)} %add.26), channel_id=1, source_target_pairs={{0,64},{8,72},{16,80},{24,88},{32,96},{40,104},{48,112},{56,120},{... | collective-permute-start | bytes 208904 | tf_op jit(solution)/shard_map/ppermute | solution.py:367
  142.0 3.2 %collective-permute-done.8 = f32[136,128]{1,0:T(8,128)S(1)} collective-permute-done((f32[136,128]{1,0:T(8,128)S(1)}, f32[136,128]{1,0:T(8,128)S(1)}, u32[]{:S(2)}, u32[]{:S(2)}) %collective-permute-start.8) | collective-permute-done | bytes 69664 | tf_op jit(solution)/shard_map/ppermute | solution.py:367
  145.3 0.5 fusion
  145.8 0.6 slice_multiply_fusion
  146.4 15.0 %all-to-all-done.3.recv_ref = bf16[8,512,256]{2,1,0:T(8,128)(2,1)S(1)} async-done(((bf16[8,512,256]{2,1,0:T(8,128)(2,1)}), bf16[8,512,256]{2,1,0:T(8,128)(2,1)S(1)}, u32[]{:S(2)}, u32[]{:S(2)}) %all-to-all-start.3) | async-done | bytes 2097184 | tf_op jit(solution)/shard_map/all_to_all | solution.py:363
  161.5 1.0 last_sum.1
  (7 shorter events, 0.1 us)
Async XLA Ops:
  3.0 7.1 %copy-start.3 = (s32[1,1,128]{2,1,0:T(1,128)S(1)}, s32[1,1,128]{2,1,0:T(1,128)}, u32[]{:S(2)}) copy-start(s32[1,1,128]{2,1,0:T(1,128)} %param.12) | copy-start | bytes 1540
  3.0 7.1 %copy-start.4 = (s32[1,1,128]{2,1,0:T(1,128)S(1)}, s32[1,1,128]{2,1,0:T(1,128)}, u32[]{:S(2)}) copy-start(s32[1,1,128]{2,1,0:T(1,128)} %param.13) | copy-start | bytes 1540
  3.0 33.4 %all-to-all-start = ((bf16[8,1024,128]{2,1,0:T(8,128)(2,1)}), bf16[8,1024,128]{2,1,0:T(8,128)(2,1)S(1)}, u32[]{:S(2)}, u32[]{:S(2)}) async-start(bf16[8,1024,128]{2,1,0:T(8,128)(2,1)} %copies.1), calls=%async_computation | async-start | bytes 4194304 | tf_op jit(solution)/shard_map/all_to_all | solution.py:363
  12.8 0.6 copy-start.1
  39.4 4.2 %collective-permute-start = (bf16[8,1024,128]{2,1,0:T(8,128)(2,1)S(1)}, bf16[8,1024,128]{2,1,0:T(8,128)(2,1)S(1)}, u32[]{:S(2)}, u32[]{:S(2)}) collective-permute-start(bf16[8,1024,128]{2,1,0:T(8,128)(2,1)S(1)} %forward_tiles.2), channel_id=1, source_target_pairs={{0,8},{8,0},{16,24},{24,16},{32,40},{40,32},{48,56},{56,48},{64,72... | collective-permute-start | bytes 6291464 | tf_op jit(solution)/shard_map/ppermute | solution.py:355
  44.1 36.1 %copy-start = (bf16[1024,128]{1,0:T(8,128)(2,1)S(1)}, bf16[1024,128]{1,0:T(8,128)(2,1)}, u32[]{:S(2)}) copy-start(bf16[1024,128]{1,0:T(8,128)(2,1)} %cot_ref.1) | copy-start | bytes 786436
  44.1 36.1 %copy-start.2 = (bf16[128,128]{1,0:T(8,128)(2,1)S(1)}, bf16[128,128]{1,0:T(8,128)(2,1)}, u32[]{:S(2)}) copy-start(bf16[128,128]{1,0:T(8,128)(2,1)} %weight_ref.1) | copy-start | bytes 98308
  44.1 36.1 %copy-start.5 = (f32[128]{0:T(128)S(1)}, f32[128]{0:T(128)}, u32[]{:S(2)}) copy-start(f32[128]{0:T(128)} %param.10) | copy-start | bytes 1540
  83.2 36.0 %all-to-all-start.2 = ((bf16[8,512,256]{2,1,0:T(8,128)(2,1)}), bf16[8,512,256]{2,1,0:T(8,128)(2,1)S(1)}, u32[]{:S(2)}, u32[]{:S(2)}) async-start(bf16[8,512,256]{2,1,0:T(8,128)(2,1)} %get-tuple-element.19), calls=%async_computation.2 | async-start | bytes 4194304 | tf_op jit(solution)/shard_map/all_to_all | solution.py:359
  87.0 4.7 %collective-permute-start.1 = (f32[136,128]{1,0:T(8,128)S(1)}, f32[136,128]{1,0:T(8,128)S(1)}, u32[]{:S(2)}, u32[]{:S(2)}) collective-permute-start(f32[136,128]{1,0:T(8,128)S(1)} %get-tuple-element.20), channel_id=1, source_target_pairs={{0,2},{1,3},{2,0},{3,1},{4,6},{5,7},{6,4},{7,5},{8,10},{9,11},{10,... | collective-permute-start | bytes 208904 | tf_op jit(solution)/shard_map/ppermute | solution.py:367
  91.7 5.9 %collective-permute-start.2 = (f32[136,128]{1,0:T(8,128)S(1)}, f32[136,128]{1,0:T(8,128)S(1)}, u32[]{:S(2)}, u32[]{:S(2)}) collective-permute-start(f32[136,128]{1,0:T(8,128)S(1)} %add.21), channel_id=1, source_target_pairs={{0,4},{1,5},{2,6},{3,7},{4,0},{5,1},{6,2},{7,3},{8,12},{9,13},{10,... | collective-permute-start | bytes 208904 | tf_op jit(solution)/shard_map/ppermute | solution.py:367
  97.6 1.3 collective-permute-start.3
  99.0 10.8 %collective-permute-start.4 = (f32[136,128]{1,0:T(8,128)S(1)}, f32[136,128]{1,0:T(8,128)S(1)}, u32[]{:S(2)}, u32[]{:S(2)}) collective-permute-start(f32[136,128]{1,0:T(8,128)S(1)} %add.23), channel_id=1, source_target_pairs={{0,1},{1,0},{2,3},{3,2},{4,5},{5,4},{6,7},{7,6},{8,9},{9,8},{10,11... | collective-permute-start | bytes 208904 | tf_op jit(solution)/shard_map/ppermute | solution.py:367
  119.3 7.0 %collective-permute-start.5 = (bf16[8,512,256]{2,1,0:T(8,128)(2,1)S(1)}, bf16[8,512,256]{2,1,0:T(8,128)(2,1)S(1)}, u32[]{:S(2)}, u32[]{:S(2)}) collective-permute-start(bf16[8,512,256]{2,1,0:T(8,128)(2,1)S(1)} %all-to-all-done.2.g), channel_id=1, source_target_pairs={{0,8},{8,0},{16,24},{24,16},{32,40},{40,32},{48,56},{56,48},{64,72... | collective-permute-start | bytes 6291464 | tf_op jit(solution)/shard_map/ppermute | solution.py:355
  119.4 11.0 %collective-permute-start.6 = (f32[136,128]{1,0:T(8,128)S(1)}, f32[136,128]{1,0:T(8,128)S(1)}, u32[]{:S(2)}, u32[]{:S(2)}) collective-permute-start(f32[136,128]{1,0:T(8,128)S(1)} %add.24), channel_id=1, source_target_pairs={{0,16},{8,24},{16,0},{24,8},{32,48},{40,56},{48,32},{56,40},{64,80... | collective-permute-start | bytes 208904 | tf_op jit(solution)/shard_map/ppermute | solution.py:367
  130.4 31.1 %all-to-all-start.3 = ((bf16[8,512,256]{2,1,0:T(8,128)(2,1)}), bf16[8,512,256]{2,1,0:T(8,128)(2,1)S(1)}, u32[]{:S(2)}, u32[]{:S(2)}) async-start(bf16[8,512,256]{2,1,0:T(8,128)(2,1)} %backward_tiles.3), calls=%async_computation.3 | async-start | bytes 4194304 | tf_op jit(solution)/shard_map/all_to_all | solution.py:363
  134.0 5.3 %collective-permute-start.7 = (f32[136,128]{1,0:T(8,128)S(1)}, f32[136,128]{1,0:T(8,128)S(1)}, u32[]{:S(2)}, u32[]{:S(2)}) collective-permute-start(f32[136,128]{1,0:T(8,128)S(1)} %add.25), channel_id=1, source_target_pairs={{0,32},{8,40},{16,48},{24,56},{32,0},{40,8},{48,16},{56,24},{64,96... | collective-permute-start | bytes 208904 | tf_op jit(solution)/shard_map/ppermute | solution.py:367
  139.4 5.9 %collective-permute-start.8 = (f32[136,128]{1,0:T(8,128)S(1)}, f32[136,128]{1,0:T(8,128)S(1)}, u32[]{:S(2)}, u32[]{:S(2)}) collective-permute-start(f32[136,128]{1,0:T(8,128)S(1)} %add.26), channel_id=1, source_target_pairs={{0,64},{8,72},{16,80},{24,88},{32,96},{40,104},{48,112},{56,120},{... | collective-permute-start | bytes 208904 | tf_op jit(solution)/shard_map/ppermute | solution.py:367

commit v2 on v1

--- a/solution.py
+++ b/solution.py
@@ -71,7 +71,7 @@
 def prep(where, out_index, in_index, count):
     return pl.pallas_call(
         prep_kernel,
-        out_shape=jax.ShapeDtypeStruct((1024,), jnp.int32),
+        out_shape=pltpu.SMEM((1024,), jnp.int32),
         in_specs=[smem()] * 4,
         out_specs=smem(),
         compiler_params=params(),
@@ -146,6 +146,10 @@
     lax.fori_loop(0, groups, body, 0)
 
 
+def in_smem(array):
+    return pltpu.with_memory_space_constraint(array, pltpu.SMEM)
+
+
 def in_hbm(array):
     return pltpu.with_memory_space_constraint(array, pltpu.HBM)
 
@@ -187,7 +191,7 @@
         compiler_params=params(),
         cost_estimate=TILES_COST,
         name="forward_tiles",
-    )(in_hbm(lists), in_hbm(values), sources)
+    )(in_smem(lists), in_hbm(values), sources)
 
 
 def pair_sum_kernel(mine_ref, other_ref, out_ref):
@@ -260,7 +264,7 @@
         compiler_params=params(),
         cost_estimate=TILES_COST,
         name="backward_tiles",
-    )(in_hbm(lists), in_hbm(values), *blocks)
+    )(in_smem(lists), in_hbm(values), *blocks)
 
 
 def dense_kernel(

time: 165 us -> 161 us (0.976)
  waiting for transfers between devices: 69.7 us -> 74.1 us
  Pallas kernels: 23.6 us -> 19.7 us
  starting transfers between devices: 29.8 us -> 28 us
    ppermute x7, starting transfers between devices: 15.8 us -> 9.13 us  [partner(): return lax.ppermute(value, axis, [(i, i ^ bit) for i in range(size)])]
    all_to_all x2, starting transfers between devices: 10 us -> 13.9 us  [col_exchange(): return lax.all_to_all(value, 'col', 0, 0)]
    all_to_all x2, waiting for transfers between devices: 38 us -> 40.4 us  [col_exchange(): return lax.all_to_all(value, 'col', 0, 0)]
    ppermute x2, waiting for transfers between devices: 0.59 us -> 2.44 us  [to_other_core(): return lax.ppermute(value, 'row', OTHER_CORE)]
    ppermute x7, waiting for transfers between devices: 21.6 us -> 23.5 us  [partner(): return lax.ppermute(value, axis, [(i, i ^ bit) for i in range(size)])]
    pallas_call x2, Pallas kernels: 7.48 us -> 5.75 us  [backward(): pl.pallas_call(functools.partial(backward_kernel, which), out_shape=jax.S...]
  transfers between devices with their start and end apart: 12 -> 12, of which waited for: 10 -> 11; matrix products, arithmetic and copies ran while one was open for 1% -> 1% of each run, Pallas kernels for 8% -> 7%
where the time goes in v2:
time: 161 us; the launch traced here: 160 us
  waiting for transfers between devices  74.1 us (46%)
  blocking collectives  35.5 us (22%)
  starting transfers between devices  28 us (17%)
  Pallas kernels  19.7 us (12%)
    all_to_all x2, waiting for transfers between devices, col_exchange(): return lax.all_to_all(value, 'col', 0, 0)  40.4 us
    all_to_all x1, blocking collectives, row_exchange(): return lax.all_to_all(value, 'row', 0, 0, axis_index_groups=SAME_CORE)  35.5 us
    ppermute x7, waiting for transfers between devices, partner(): return lax.ppermute(value, axis, [(i, i ^ bit) for i in range(size)])  23.5 us
    all_to_all x2, starting transfers between devices, col_exchange(): return lax.all_to_all(value, 'col', 0, 0)  13.9 us
    ppermute x7, starting transfers between devices, partner(): return lax.ppermute(value, axis, [(i, i ^ bit) for i in range(size)])  9.13 us
    all_to_all x1, waiting for transfers between devices, row_exchange(): return lax.all_to_all(value, 'row', 0, 0, axis_index_groups=SAME_CORE)  7.87 us
    pallas_call x2, Pallas kernels, backward(): pl.pallas_call(functools.partial(backward_kernel, which), out_shape=jax.S...  5.75 us
    pallas_call x2, Pallas kernels, forward(): pl.pallas_call(functools.partial(forward_kernel, which), out_shape=jax.Sh...  4.86 us
  transfers between devices with their start and end apart: 12, of which 11 were waited for; matrix products, arithmetic and copies ran while one was open for 1% of the time, Pallas kernels for 7%

profile of v2, /device:TPU:0, one launch (start us, length us, event | category | flops | bytes accessed | tf_op | source)
XLA Modules:
  0.0 160.1 jit_solution(2202870553461557471)
XLA Ops:
  0.6 2.4 %copies.1 = bf16[8,1024,128]{2,1,0:T(8,128)(2,1)} custom-call(bf16[1024,128]{1,0:T(8,128)(2,1)} %value_ref.1), custom_call_target="tpu_custom_call" | custom-call | tf_op jit(solution)/shard_map/copies/pallas_call | solution.py:94
  3.0 0.0 copy-start.2
  3.0 0.0 copy-start.3
  3.0 6.4 %all-to-all-start = ((bf16[8,1024,128]{2,1,0:T(8,128)(2,1)}), bf16[8,1024,128]{2,1,0:T(8,128)(2,1)S(1)}, u32[]{:S(2)}, u32[]{:S(2)}) async-start(bf16[8,1024,128]{2,1,0:T(8,128)(2,1)} %copies.1), calls=%async_computation | async-start | bytes 4194304 | tf_op jit(solution)/shard_map/all_to_all | solution.py:367
  10.1 0.0 copy-done.2
  10.1 0.0 copy-done.3
  10.1 2.1 %slot_lists.1.lists_ref = s32[1024]{0:T(1024)S(4)} custom-call(s32[1]{0:T(128)} %bitcast.where_ref, s32[128]{0:T(128)S(1)} %bitcast.9, s32[128]{0:T(128)S(1)} %bitcast.10, s32[1]{0:T(128)} %bitcast.8.count_ref), custom_call_target="tpu_custom_call" | custom-call | tf_op jit(solution)/shard_map/slot_lists/pallas_call | solution.py:72
  12.2 24.2 %all-to-all-done.x = bf16[8,1024,128]{2,1,0:T(8,128)(2,1)S(1)} async-done(((bf16[8,1024,128]{2,1,0:T(8,128)(2,1)}), bf16[8,1024,128]{2,1,0:T(8,128)(2,1)S(1)}, u32[]{:S(2)}, u32[]{:S(2)}) %all-to-all-start) | async-done | bytes 2097184 | tf_op jit(solution)/shard_map/all_to_all | solution.py:367
  36.4 2.2 %forward_tiles.2 = bf16[8,1024,128]{2,1,0:T(8,128)(2,1)S(1)} custom-call(s32[1024]{0:T(1024)S(4)} %slot_lists.1.lists_ref, bf16[128,256,256]{2,1,0:T(8,128)(2,1)} %bitcast.12, bf16[8,1024,128]{2,1,0:T(8,128)(2,1)S(1)} %all-to-all-done.x), custom_call_target="tpu_custom_call" | custom-call | flops 1073741824 | bytes 16777216 | tf_op jit(solution)/shard_map/forward_tiles/pallas_call | solution.py:181
  38.6 1.4 collective-permute-start
  40.1 2.7 %forward_tiles.3.mine_ref = bf16[8,1024,128]{2,1,0:T(8,128)(2,1)S(1)} custom-call(s32[1024]{0:T(1024)S(4)} %slot_lists.1.lists_ref, bf16[128,256,256]{2,1,0:T(8,128)(2,1)} %bitcast.13, bf16[8,1024,128]{2,1,0:T(8,128)(2,1)S(1)} %all-to-all-done.x), custom_call_target="tpu_custom_call" | custom-call | flops 1073741824 | bytes 16777216 | tf_op jit(solution)/shard_map/forward_tiles/pallas_call | solution.py:181
  42.7 1.1 collective-permute-done.other_ref
  43.9 0.5 pair_sum.1
  44.3 0.0 copy-start
  44.3 0.0 copy-start.1
  44.4 0.0 copy-start.4
  44.4 35.5 %all_to_all.20.recv_ref = bf16[8,1024,128]{2,1,0:T(8,128)(2,1)S(1)} all-to-all(bf16[8,1024,128]{2,1,0:T(8,128)(2,1)S(1)} %pair_sum.1), channel_id=1, replica_groups={{0,16,32,48,64,80,96,112},{8,24,40,56,72,88,104,120},{1,17,33,49,65,81,..., dimensions={0} | all-to-all | bytes 4194304 | tf_op jit(solution)/shard_map/all_to_all | solution.py:363
  79.9 0.0 copy-done
  79.9 0.0 copy-done.1
  79.9 0.0 copy-done.4
  79.9 3.1 %dense_layer.1 = (bf16[1024,128]{1,0:T(8,128)(2,1)}, bf16[8,512,256]{2,1,0:T(8,128)(2,1)}, f32[136,128]{1,0:T(8,128)S(1)}) custom-call(bf16[8,1024,128]{2,1,0:T(8,128)(2,1)S(1)} %all_to_all.20.recv_ref, bf16[128,128]{1,0:T(8,128)(2,1)S(1)} %copy-done.1, f32[1,128]{1,0:T(1,128)S(1)} %bitcast.11, bf16[1024,128]{1,0:T(8,128)(2,1)S(1)} %copy-done), custom_call_target="tpu_custom_call" | custom-call | flops 100663296 | bytes 5242880 | tf_op jit(solution)/shard_map/dense_layer/pallas_call | solution.py:312
  83.0 3.6 %all-to-all-start.2 = ((bf16[8,512,256]{2,1,0:T(8,128)(2,1)}), bf16[8,512,256]{2,1,0:T(8,128)(2,1)S(1)}, u32[]{:S(2)}, u32[]{:S(2)}) async-start(bf16[8,512,256]{2,1,0:T(8,128)(2,1)} %get-tuple-element.19), calls=%async_computation.2 | async-start | bytes 4194304 | tf_op jit(solution)/shard_map/all_to_all | solution.py:363
  86.6 1.0 collective-permute-start.1
  87.6 3.4 %collective-permute-done.1 = f32[136,128]{1,0:T(8,128)S(1)} collective-permute-done((f32[136,128]{1,0:T(8,128)S(1)}, f32[136,128]{1,0:T(8,128)S(1)}, u32[]{:S(2)}, u32[]{:S(2)}) %collective-permute-start.1) | collective-permute-done | bytes 69664 | tf_op jit(solution)/shard_map/ppermute | solution.py:371
  91.0 2.3 %collective-permute-start.2 = (f32[136,128]{1,0:T(8,128)S(1)}, f32[136,128]{1,0:T(8,128)S(1)}, u32[]{:S(2)}, u32[]{:S(2)}) collective-permute-start(f32[136,128]{1,0:T(8,128)S(1)} %add.21), channel_id=1, source_target_pairs={{0,4},{1,5},{2,6},{3,7},{4,0},{5,1},{6,2},{7,3},{8,12},{9,13},{10,... | collective-permute-start | bytes 208904 | tf_op jit(solution)/shard_map/ppermute | solution.py:371
  93.3 3.6 %collective-permute-done.2 = f32[136,128]{1,0:T(8,128)S(1)} collective-permute-done((f32[136,128]{1,0:T(8,128)S(1)}, f32[136,128]{1,0:T(8,128)S(1)}, u32[]{:S(2)}, u32[]{:S(2)}) %collective-permute-start.2) | collective-permute-done | bytes 69664 | tf_op jit(solution)/shard_map/ppermute | solution.py:371
  96.9 0.1 collective-permute-start.3
  97.0 1.2 collective-permute-done.3
  98.3 0.9 collective-permute-start.4
  99.2 9.0 %collective-permute-done.4 = f32[136,128]{1,0:T(8,128)S(1)} collective-permute-done((f32[136,128]{1,0:T(8,128)S(1)}, f32[136,128]{1,0:T(8,128)S(1)}, u32[]{:S(2)}, u32[]{:S(2)}) %collective-permute-start.4) | collective-permute-done | bytes 69664 | tf_op jit(solution)/shard_map/ppermute | solution.py:371
  108.2 7.9 %all-to-all-done.2.g = bf16[8,512,256]{2,1,0:T(8,128)(2,1)S(1)} async-done(((bf16[8,512,256]{2,1,0:T(8,128)(2,1)}), bf16[8,512,256]{2,1,0:T(8,128)(2,1)S(1)}, u32[]{:S(2)}, u32[]{:S(2)}) %all-to-all-start.2) | async-done | bytes 2097184 | tf_op jit(solution)/shard_map/all_to_all | solution.py:363
  116.1 0.0 collective-permute-start.5
  116.1 0.4 collective-permute-start.6
  116.5 2.4 %backward_tiles.2.rest_0_ = bf16[8,512,256]{2,1,0:T(8,128)(2,1)S(1)} custom-call(s32[1024]{0:T(1024)S(4)} %slot_lists.1.lists_ref, bf16[128,256,256]{2,1,0:T(8,128)(2,1)} %bitcast.14, bf16[8,512,256]{2,1,0:T(8,128)(2,1)S(1)} %all-to-all-done.2.g), custom_call_target="tpu_custom_call" | custom-call | flops 1073741824 | bytes 16777216 | tf_op jit(solution)/shard_map/backward_tiles/pallas_call | solution.py:258
  118.9 1.3 collective-permute-done.5.g
  120.2 3.3 %backward_tiles.3 = bf16[8,512,256]{2,1,0:T(8,128)(2,1)} custom-call(s32[1024]{0:T(1024)S(4)} %slot_lists.1.lists_ref, bf16[128,256,256]{2,1,0:T(8,128)(2,1)} %bitcast.15, bf16[8,512,256]{2,1,0:T(8,128)(2,1)S(1)} %collective-permute-done.5.g, bf16[8,512,256]{2,1,0:T(8,128)(2,1)S(1)} %backward_tiles.2.rest_0_), custom_call_target="tpu_custom_call" | custom-call | flops 1073741824 | bytes 16777216 | tf_op jit(solution)/shard_map/backward_tiles/pallas_call | solution.py:258
  123.6 0.0 collective-permute-done.6
  123.6 7.4 %all-to-all-start.3 = ((bf16[8,512,256]{2,1,0:T(8,128)(2,1)}), bf16[8,512,256]{2,1,0:T(8,128)(2,1)S(1)}, u32[]{:S(2)}, u32[]{:S(2)}) async-start(bf16[8,512,256]{2,1,0:T(8,128)(2,1)} %backward_tiles.3), calls=%async_computation.3 | async-start | bytes 4194304 | tf_op jit(solution)/shard_map/all_to_all | solution.py:367
  131.0 2.4 %collective-permute-start.7 = (f32[136,128]{1,0:T(8,128)S(1)}, f32[136,128]{1,0:T(8,128)S(1)}, u32[]{:S(2)}, u32[]{:S(2)}) collective-permute-start(f32[136,128]{1,0:T(8,128)S(1)} %add.25), channel_id=1, source_target_pairs={{0,32},{8,40},{16,48},{24,56},{32,0},{40,8},{48,16},{56,24},{64,96... | collective-permute-start | bytes 208904 | tf_op jit(solution)/shard_map/ppermute | solution.py:371
  133.5 2.3 %collective-permute-done.7 = f32[136,128]{1,0:T(8,128)S(1)} collective-permute-done((f32[136,128]{1,0:T(8,128)S(1)}, f32[136,128]{1,0:T(8,128)S(1)}, u32[]{:S(2)}, u32[]{:S(2)}) %collective-permute-start.7) | collective-permute-done | bytes 69664 | tf_op jit(solution)/shard_map/ppermute | solution.py:371
  135.8 2.1 %collective-permute-start.8 = (f32[136,128]{1,0:T(8,128)S(1)}, f32[136,128]{1,0:T(8,128)S(1)}, u32[]{:S(2)}, u32[]{:S(2)}) collective-permute-start(f32[136,128]{1,0:T(8,128)S(1)} %add.26), channel_id=1, source_target_pairs={{0,64},{8,72},{16,80},{24,88},{32,96},{40,104},{48,112},{56,120},{... | collective-permute-start | bytes 208904 | tf_op jit(solution)/shard_map/ppermute | solution.py:371
  137.9 3.8 %collective-permute-done.8 = f32[136,128]{1,0:T(8,128)S(1)} collective-permute-done((f32[136,128]{1,0:T(8,128)S(1)}, f32[136,128]{1,0:T(8,128)S(1)}, u32[]{:S(2)}, u32[]{:S(2)}) %collective-permute-start.8) | collective-permute-done | bytes 69664 | tf_op jit(solution)/shard_map/ppermute | solution.py:371
  141.7 0.5 fusion
  142.2 0.6 slice_multiply_fusion
  142.9 16.2 %all-to-all-done.3.recv_ref = bf16[8,512,256]{2,1,0:T(8,128)(2,1)S(1)} async-done(((bf16[8,512,256]{2,1,0:T(8,128)(2,1)}), bf16[8,512,256]{2,1,0:T(8,128)(2,1)S(1)}, u32[]{:S(2)}, u32[]{:S(2)}) %all-to-all-start.3) | async-done | bytes 2097184 | tf_op jit(solution)/shard_map/all_to_all | solution.py:367
  159.0 1.0 last_sum.1
  (7 shorter events, 0.1 us)
Async XLA Ops:
  3.0 7.1 %copy-start.2 = (s32[1,1,128]{2,1,0:T(1,128)S(1)}, s32[1,1,128]{2,1,0:T(1,128)}, u32[]{:S(2)}) copy-start(s32[1,1,128]{2,1,0:T(1,128)} %param.12) | copy-start | bytes 1540
  3.0 7.1 %copy-start.3 = (s32[1,1,128]{2,1,0:T(1,128)S(1)}, s32[1,1,128]{2,1,0:T(1,128)}, u32[]{:S(2)}) copy-start(s32[1,1,128]{2,1,0:T(1,128)} %param.13) | copy-start | bytes 1540
  3.0 33.4 %all-to-all-start = ((bf16[8,1024,128]{2,1,0:T(8,128)(2,1)}), bf16[8,1024,128]{2,1,0:T(8,128)(2,1)S(1)}, u32[]{:S(2)}, u32[]{:S(2)}) async-start(bf16[8,1024,128]{2,1,0:T(8,128)(2,1)} %copies.1), calls=%async_computation | async-start | bytes 4194304 | tf_op jit(solution)/shard_map/all_to_all | solution.py:367
  38.6 5.2 %collective-permute-start = (bf16[8,1024,128]{2,1,0:T(8,128)(2,1)S(1)}, bf16[8,1024,128]{2,1,0:T(8,128)(2,1)S(1)}, u32[]{:S(2)}, u32[]{:S(2)}) collective-permute-start(bf16[8,1024,128]{2,1,0:T(8,128)(2,1)S(1)} %forward_tiles.2), channel_id=1, source_target_pairs={{0,8},{8,0},{16,24},{24,16},{32,40},{40,32},{48,56},{56,48},{64,72... | collective-permute-start | bytes 6291464 | tf_op jit(solution)/shard_map/ppermute | solution.py:359
  44.3 35.6 %copy-start = (bf16[1024,128]{1,0:T(8,128)(2,1)S(1)}, bf16[1024,128]{1,0:T(8,128)(2,1)}, u32[]{:S(2)}) copy-start(bf16[1024,128]{1,0:T(8,128)(2,1)} %cot_ref.1) | copy-start | bytes 786436
  44.3 35.5 %copy-start.1 = (bf16[128,128]{1,0:T(8,128)(2,1)S(1)}, bf16[128,128]{1,0:T(8,128)(2,1)}, u32[]{:S(2)}) copy-start(bf16[128,128]{1,0:T(8,128)(2,1)} %weight_ref.1) | copy-start | bytes 98308
  44.4 35.5 %copy-start.4 = (f32[128]{0:T(128)S(1)}, f32[128]{0:T(128)}, u32[]{:S(2)}) copy-start(f32[128]{0:T(128)} %param.10) | copy-start | bytes 1540
  83.0 33.1 %all-to-all-start.2 = ((bf16[8,512,256]{2,1,0:T(8,128)(2,1)}), bf16[8,512,256]{2,1,0:T(8,128)(2,1)S(1)}, u32[]{:S(2)}, u32[]{:S(2)}) async-start(bf16[8,512,256]{2,1,0:T(8,128)(2,1)} %get-tuple-element.19), calls=%async_computation.2 | async-start | bytes 4194304 | tf_op jit(solution)/shard_map/all_to_all | solution.py:363
  86.6 4.4 %collective-permute-start.1 = (f32[136,128]{1,0:T(8,128)S(1)}, f32[136,128]{1,0:T(8,128)S(1)}, u32[]{:S(2)}, u32[]{:S(2)}) collective-permute-start(f32[136,128]{1,0:T(8,128)S(1)} %get-tuple-element.20), channel_id=1, source_target_pairs={{0,2},{1,3},{2,0},{3,1},{4,6},{5,7},{6,4},{7,5},{8,10},{9,11},{10,... | collective-permute-start | bytes 208904 | tf_op jit(solution)/shard_map/ppermute | solution.py:371
  91.0 5.9 %collective-permute-start.2 = (f32[136,128]{1,0:T(8,128)S(1)}, f32[136,128]{1,0:T(8,128)S(1)}, u32[]{:S(2)}, u32[]{:S(2)}) collective-permute-start(f32[136,128]{1,0:T(8,128)S(1)} %add.21), channel_id=1, source_target_pairs={{0,4},{1,5},{2,6},{3,7},{4,0},{5,1},{6,2},{7,3},{8,12},{9,13},{10,... | collective-permute-start | bytes 208904 | tf_op jit(solution)/shard_map/ppermute | solution.py:371
  96.9 1.3 collective-permute-start.3
  98.3 9.9 %collective-permute-start.4 = (f32[136,128]{1,0:T(8,128)S(1)}, f32[136,128]{1,0:T(8,128)S(1)}, u32[]{:S(2)}, u32[]{:S(2)}) collective-permute-start(f32[136,128]{1,0:T(8,128)S(1)} %add.23), channel_id=1, source_target_pairs={{0,1},{1,0},{2,3},{3,2},{4,5},{5,4},{6,7},{7,6},{8,9},{9,8},{10,11... | collective-permute-start | bytes 208904 | tf_op jit(solution)/shard_map/ppermute | solution.py:371
  116.1 4.2 %collective-permute-start.5 = (bf16[8,512,256]{2,1,0:T(8,128)(2,1)S(1)}, bf16[8,512,256]{2,1,0:T(8,128)(2,1)S(1)}, u32[]{:S(2)}, u32[]{:S(2)}) collective-permute-start(bf16[8,512,256]{2,1,0:T(8,128)(2,1)S(1)} %all-to-all-done.2.g), channel_id=1, source_target_pairs={{0,8},{8,0},{16,24},{24,16},{32,40},{40,32},{48,56},{56,48},{64,72... | collective-permute-start | bytes 6291464 | tf_op jit(solution)/shard_map/ppermute | solution.py:359
  116.1 7.5 %collective-permute-start.6 = (f32[136,128]{1,0:T(8,128)S(1)}, f32[136,128]{1,0:T(8,128)S(1)}, u32[]{:S(2)}, u32[]{:S(2)}) collective-permute-start(f32[136,128]{1,0:T(8,128)S(1)} %add.24), channel_id=1, source_target_pairs={{0,16},{8,24},{16,0},{24,8},{32,48},{40,56},{48,32},{56,40},{64,80... | collective-permute-start | bytes 208904 | tf_op jit(solution)/shard_map/ppermute | solution.py:371
  123.6 35.5 %all-to-all-start.3 = ((bf16[8,512,256]{2,1,0:T(8,128)(2,1)}), bf16[8,512,256]{2,1,0:T(8,128)(2,1)S(1)}, u32[]{:S(2)}, u32[]{:S(2)}) async-start(bf16[8,512,256]{2,1,0:T(8,128)(2,1)} %backward_tiles.3), calls=%async_computation.3 | async-start | bytes 4194304 | tf_op jit(solution)/shard_map/all_to_all | solution.py:367
  131.0 4.8 %collective-permute-start.7 = (f32[136,128]{1,0:T(8,128)S(1)}, f32[136,128]{1,0:T(8,128)S(1)}, u32[]{:S(2)}, u32[]{:S(2)}) collective-permute-start(f32[136,128]{1,0:T(8,128)S(1)} %add.25), channel_id=1, source_target_pairs={{0,32},{8,40},{16,48},{24,56},{32,0},{40,8},{48,16},{56,24},{64,96... | collective-permute-start | bytes 208904 | tf_op jit(solution)/shard_map/ppermute | solution.py:371
  135.8 5.9 %collective-permute-start.8 = (f32[136,128]{1,0:T(8,128)S(1)}, f32[136,128]{1,0:T(8,128)S(1)}, u32[]{:S(2)}, u32[]{:S(2)}) collective-permute-start(f32[136,128]{1,0:T(8,128)S(1)} %add.26), channel_id=1, source_target_pairs={{0,64},{8,72},{16,80},{24,88},{32,96},{40,104},{48,112},{56,120},{... | collective-permute-start | bytes 208904 | tf_op jit(solution)/shard_map/ppermute | solution.py:371

commit v3 on v2

--- a/solution.py
+++ b/solution.py
@@ -389,14 +389,13 @@
     for bit in (2, 4):
         total = total + partner(total, "col", 8, bit)
     total = total + partner(total, "row", 16, 1)
-    total = total + partner(total, "col", 8, 1)
+    both = [(r * 8 + c, (r ^ 2) * 8 + (c ^ 1)) for r in range(16) for c in range(8)]
+    near, far = partner(total, "col", 8, 1), partner(total, "row", 16, 2)
+    total = (total + near) + (far + lax.ppermute(total, ("row", "col"), both))
     grads, total = order((grads, total))
     other = to_other_core(grads)
-    second = partner(total, "row", 16, 2)
     back = backward(2, lists, values, grads)
     back = backward(3, lists, values, other, back)
-    back, second = order((back, second))
-    total = total + second
     back = col_exchange(back)
     for bit in (4, 8):
         total = total + partner(total, "row", 16, bit)

time: 161 us -> 159 us (0.988)
  Pallas kernels: 19.7 us -> 29.4 us
  starting transfers between devices: 28 us -> 20 us
  waiting for transfers between devices: 74.1 us -> 70.1 us
    ppermute x7, waiting for transfers between devices: 23.5 us -> 31 us  [partner(): return lax.ppermute(value, axis, [(i, i ^ bit) for i in range(size)])]
    all_to_all x1, waiting for transfers between devices: 7.87 us -> 0.77 us  [row_exchange(): return lax.all_to_all(value, 'row', 0, 0, axis_index_groups=SAME_CORE)]
    pallas_call x2, Pallas kernels: 4.86 us -> 9.51 us  [forward(): pl.pallas_call(functools.partial(forward_kernel, which), out_shape=jax.Sh...]
    pallas_call x2, Pallas kernels: 5.75 us -> 9.77 us  [backward(): pl.pallas_call(functools.partial(backward_kernel, which), out_shape=jax.S...]
    ppermute x7, starting transfers between devices: 9.13 us -> 5.34 us  [partner(): return lax.ppermute(value, axis, [(i, i ^ bit) for i in range(size)])]
    all_to_all x2, waiting for transfers between devices: 40.4 us -> 37 us  [col_exchange(): return lax.all_to_all(value, 'col', 0, 0)]
    all_to_all x2, starting transfers between devices: 13.9 us -> 11 us  [col_exchange(): return lax.all_to_all(value, 'col', 0, 0)]
    ppermute x2, waiting for transfers between devices: 2.44 us -> 0.01 us  [to_other_core(): return lax.ppermute(value, 'row', OTHER_CORE)]
  transfers between devices with their start and end apart: 12 -> 13, of which waited for: 11 -> 10; matrix products, arithmetic and copies ran while one was open for 1% -> 1% of each run, Pallas kernels for 7% -> 8%
where the time goes in v3:
time: 159 us; the launch traced here: 158 us
  waiting for transfers between devices  70.1 us (44%)
  blocking collectives  35.2 us (22%)
  Pallas kernels  29.4 us (18%)
  starting transfers between devices  20 us (13%)
    all_to_all x2, waiting for transfers between devices, col_exchange(): return lax.all_to_all(value, 'col', 0, 0)  37 us
    all_to_all x1, blocking collectives, row_exchange(): return lax.all_to_all(value, 'row', 0, 0, axis_index_groups=SAME_CORE)  35.2 us
    ppermute x7, waiting for transfers between devices, partner(): return lax.ppermute(value, axis, [(i, i ^ bit) for i in range(size)])  31 us
    all_to_all x2, starting transfers between devices, col_exchange(): return lax.all_to_all(value, 'col', 0, 0)  11 us
    pallas_call x2, Pallas kernels, backward(): pl.pallas_call(functools.partial(backward_kernel, which), out_shape=jax.S...  9.77 us
    pallas_call x2, Pallas kernels, forward(): pl.pallas_call(functools.partial(forward_kernel, which), out_shape=jax.Sh...  9.51 us
    ppermute x7, starting transfers between devices, partner(): return lax.ppermute(value, axis, [(i, i ^ bit) for i in range(size)])  5.34 us
    all_to_all x1, starting transfers between devices, row_exchange(): return lax.all_to_all(value, 'row', 0, 0, axis_index_groups=SAME_CORE)  3.61 us
  transfers between devices with their start and end apart: 13, of which 10 were waited for; matrix products, arithmetic and copies ran while one was open for 1% of the time, Pallas kernels for 8%

profile of v3, /device:TPU:0, one launch (start us, length us, event | category | flops | bytes accessed | tf_op | source)
XLA Modules:
  0.0 157.5 jit_solution(10095162524837544619)
XLA Ops:
  0.6 2.4 %copies.1 = bf16[8,1024,128]{2,1,0:T(8,128)(2,1)} custom-call(bf16[1024,128]{1,0:T(8,128)(2,1)} %value_ref.1), custom_call_target="tpu_custom_call" | custom-call | tf_op jit(solution)/shard_map/copies/pallas_call | solution.py:94
  3.0 0.0 copy-start.2
  3.0 0.0 copy-start.3
  3.0 6.4 %all-to-all-start = ((bf16[8,1024,128]{2,1,0:T(8,128)(2,1)}), bf16[8,1024,128]{2,1,0:T(8,128)(2,1)S(1)}, u32[]{:S(2)}, u32[]{:S(2)}) async-start(bf16[8,1024,128]{2,1,0:T(8,128)(2,1)} %copies.1), calls=%async_computation | async-start | bytes 4194304 | tf_op jit(solution)/shard_map/all_to_all | solution.py:367
  10.1 0.0 copy-done.2
  10.1 0.0 copy-done.3
  10.1 3.3 %slot_lists.1.lists_ref = s32[1024]{0:T(1024)S(4)} custom-call(s32[1]{0:T(128)} %bitcast.where_ref, s32[128]{0:T(128)S(1)} %bitcast.9, s32[128]{0:T(128)S(1)} %bitcast.10, s32[1]{0:T(128)} %bitcast.8.count_ref), custom_call_target="tpu_custom_call" | custom-call | tf_op jit(solution)/shard_map/slot_lists/pallas_call | solution.py:72
  13.4 23.0 %all-to-all-done.x = bf16[8,1024,128]{2,1,0:T(8,128)(2,1)S(1)} async-done(((bf16[8,1024,128]{2,1,0:T(8,128)(2,1)}), bf16[8,1024,128]{2,1,0:T(8,128)(2,1)S(1)}, u32[]{:S(2)}, u32[]{:S(2)}) %all-to-all-start) | async-done | bytes 2097184 | tf_op jit(solution)/shard_map/all_to_all | solution.py:367
  36.4 4.5 %forward_tiles.2 = bf16[8,1024,128]{2,1,0:T(8,128)(2,1)S(1)} custom-call(s32[1024]{0:T(1024)S(4)} %slot_lists.1.lists_ref, bf16[128,256,256]{2,1,0:T(8,128)(2,1)} %bitcast.12, bf16[8,1024,128]{2,1,0:T(8,128)(2,1)S(1)} %all-to-all-done.x), custom_call_target="tpu_custom_call" | custom-call | flops 1073741824 | bytes 16777216 | tf_op jit(solution)/shard_map/forward_tiles/pallas_call | solution.py:181
  40.9 0.1 collective-permute-start
  41.0 5.0 %forward_tiles.3.mine_ref = bf16[8,1024,128]{2,1,0:T(8,128)(2,1)S(1)} custom-call(s32[1024]{0:T(1024)S(4)} %slot_lists.1.lists_ref, bf16[128,256,256]{2,1,0:T(8,128)(2,1)} %bitcast.13, bf16[8,1024,128]{2,1,0:T(8,128)(2,1)S(1)} %all-to-all-done.x), custom_call_target="tpu_custom_call" | custom-call | flops 1073741824 | bytes 16777216 | tf_op jit(solution)/shard_map/forward_tiles/pallas_call | solution.py:181
  46.0 0.0 collective-permute-done.other_ref
  46.0 0.5 pair_sum.1
  46.5 0.0 copy-start
  46.5 0.0 copy-start.1
  46.6 0.0 copy-start.4
  46.6 35.2 %all_to_all.20.recv_ref = bf16[8,1024,128]{2,1,0:T(8,128)(2,1)S(1)} all-to-all(bf16[8,1024,128]{2,1,0:T(8,128)(2,1)S(1)} %pair_sum.1), channel_id=1, replica_groups={{0,16,32,48,64,80,96,112},{8,24,40,56,72,88,104,120},{1,17,33,49,65,81,..., dimensions={0} | all-to-all | bytes 4194304 | tf_op jit(solution)/shard_map/all_to_all | solution.py:363
  81.8 0.0 copy-done
  81.8 0.0 copy-done.1
  81.8 0.0 copy-done.4
  81.8 3.0 %dense_layer.1 = (bf16[1024,128]{1,0:T(8,128)(2,1)}, bf16[8,512,256]{2,1,0:T(8,128)(2,1)}, f32[136,128]{1,0:T(8,128)S(1)}) custom-call(bf16[8,1024,128]{2,1,0:T(8,128)(2,1)S(1)} %all_to_all.20.recv_ref, bf16[128,128]{1,0:T(8,128)(2,1)S(1)} %copy-done.1, f32[1,128]{1,0:T(1,128)S(1)} %bitcast.11, bf16[1024,128]{1,0:T(8,128)(2,1)S(1)} %copy-done), custom_call_target="tpu_custom_call" | custom-call | flops 100663296 | bytes 5242880 | tf_op jit(solution)/shard_map/dense_layer/pallas_call | solution.py:312
  84.9 3.6 %all-to-all-start.2 = ((bf16[8,512,256]{2,1,0:T(8,128)(2,1)}), bf16[8,512,256]{2,1,0:T(8,128)(2,1)S(1)}, u32[]{:S(2)}, u32[]{:S(2)}) async-start(bf16[8,512,256]{2,1,0:T(8,128)(2,1)} %get-tuple-element.17), calls=%async_computation.2 | async-start | bytes 4194304 | tf_op jit(solution)/shard_map/all_to_all | solution.py:363
  88.5 0.1 collective-permute-start.1
  88.6 4.3 %collective-permute-done.1 = f32[136,128]{1,0:T(8,128)S(1)} collective-permute-done((f32[136,128]{1,0:T(8,128)S(1)}, f32[136,128]{1,0:T(8,128)S(1)}, u32[]{:S(2)}, u32[]{:S(2)}) %collective-permute-start.1) | collective-permute-done | bytes 69664 | tf_op jit(solution)/shard_map/ppermute | solution.py:371
  92.9 0.2 collective-permute-start.2
  93.1 5.7 %collective-permute-done.2 = f32[136,128]{1,0:T(8,128)S(1)} collective-permute-done((f32[136,128]{1,0:T(8,128)S(1)}, f32[136,128]{1,0:T(8,128)S(1)}, u32[]{:S(2)}, u32[]{:S(2)}) %collective-permute-start.2) | collective-permute-done | bytes 69664 | tf_op jit(solution)/shard_map/ppermute | solution.py:371
  98.8 0.1 collective-permute-start.3
  98.9 1.2 collective-permute-done.3
  100.1 3.4 %collective-permute-start.5 = (f32[136,128]{1,0:T(8,128)S(1)}, f32[136,128]{1,0:T(8,128)S(1)}, u32[]{:S(2)}, u32[]{:S(2)}) collective-permute-start(f32[136,128]{1,0:T(8,128)S(1)} %add.26), channel_id=1, source_target_pairs={{0,16},{8,24},{16,0},{24,8},{32,48},{40,56},{48,32},{56,40},{64,80... | collective-permute-start | bytes 208904 | tf_op jit(solution)/shard_map/ppermute | solution.py:371
  103.6 0.0 collective-permute-start.6
  103.6 0.1 collective-permute-start.4
  103.7 11.0 %collective-permute-done.5 = f32[136,128]{1,0:T(8,128)S(1)} collective-permute-done((f32[136,128]{1,0:T(8,128)S(1)}, f32[136,128]{1,0:T(8,128)S(1)}, u32[]{:S(2)}, u32[]{:S(2)}) %collective-permute-start.5) | collective-permute-done | bytes 69664 | tf_op jit(solution)/shard_map/ppermute | solution.py:371
  114.7 1.3 collective-permute-done.6
  116.0 0.0 collective-permute-done.4
  116.0 0.8 all-to-all-done.2.g
  116.8 0.0 collective-permute-start.7
  116.8 4.5 %backward_tiles.2.rest_0_ = bf16[8,512,256]{2,1,0:T(8,128)(2,1)S(1)} custom-call(s32[1024]{0:T(1024)S(4)} %slot_lists.1.lists_ref, bf16[128,256,256]{2,1,0:T(8,128)(2,1)} %bitcast.14, bf16[8,512,256]{2,1,0:T(8,128)(2,1)S(1)} %all-to-all-done.2.g), custom_call_target="tpu_custom_call" | custom-call | flops 1073741824 | bytes 16777216 | tf_op jit(solution)/shard_map/backward_tiles/pallas_call | solution.py:258
  121.3 0.0 collective-permute-done.7.g
  121.3 5.2 %backward_tiles.3 = bf16[8,512,256]{2,1,0:T(8,128)(2,1)} custom-call(s32[1024]{0:T(1024)S(4)} %slot_lists.1.lists_ref, bf16[128,256,256]{2,1,0:T(8,128)(2,1)} %bitcast.15, bf16[8,512,256]{2,1,0:T(8,128)(2,1)S(1)} %collective-permute-done.7.g, bf16[8,512,256]{2,1,0:T(8,128)(2,1)S(1)} %backward_tiles.2.rest_0_), custom_call_target="tpu_custom_call" | custom-call | flops 1073741824 | bytes 16777216 | tf_op jit(solution)/shard_map/backward_tiles/pallas_call | solution.py:258
  126.6 4.6 %all-to-all-start.3 = ((bf16[8,512,256]{2,1,0:T(8,128)(2,1)}), bf16[8,512,256]{2,1,0:T(8,128)(2,1)S(1)}, u32[]{:S(2)}, u32[]{:S(2)}) async-start(bf16[8,512,256]{2,1,0:T(8,128)(2,1)} %backward_tiles.3), calls=%async_computation.3 | async-start | bytes 4194304 | tf_op jit(solution)/shard_map/all_to_all | solution.py:367
  131.1 0.2 collective-permute-start.8
  131.3 4.1 %collective-permute-done.8 = f32[136,128]{1,0:T(8,128)S(1)} collective-permute-done((f32[136,128]{1,0:T(8,128)S(1)}, f32[136,128]{1,0:T(8,128)S(1)}, u32[]{:S(2)}, u32[]{:S(2)}) %collective-permute-start.8) | collective-permute-done | bytes 69664 | tf_op jit(solution)/shard_map/ppermute | solution.py:371
  135.4 1.2 collective-permute-start.9
  136.7 4.7 %collective-permute-done.9 = f32[136,128]{1,0:T(8,128)S(1)} collective-permute-done((f32[136,128]{1,0:T(8,128)S(1)}, f32[136,128]{1,0:T(8,128)S(1)}, u32[]{:S(2)}, u32[]{:S(2)}) %collective-permute-start.9) | collective-permute-done | bytes 69664 | tf_op jit(solution)/shard_map/ppermute | solution.py:371
  141.4 0.5 fusion
  141.9 0.6 slice_multiply_fusion
  142.5 14.0 %all-to-all-done.3.recv_ref = bf16[8,512,256]{2,1,0:T(8,128)(2,1)S(1)} async-done(((bf16[8,512,256]{2,1,0:T(8,128)(2,1)}), bf16[8,512,256]{2,1,0:T(8,128)(2,1)S(1)}, u32[]{:S(2)}, u32[]{:S(2)}) %all-to-all-start.3) | async-done | bytes 2097184 | tf_op jit(solution)/shard_map/all_to_all | solution.py:367
  156.5 1.0 last_sum.1
  (6 shorter events, 0.1 us)
Async XLA Ops:
  3.0 7.1 %copy-start.2 = (s32[1,1,128]{2,1,0:T(1,128)S(1)}, s32[1,1,128]{2,1,0:T(1,128)}, u32[]{:S(2)}) copy-start(s32[1,1,128]{2,1,0:T(1,128)} %param.12) | copy-start | bytes 1540
  3.0 7.1 %copy-start.3 = (s32[1,1,128]{2,1,0:T(1,128)S(1)}, s32[1,1,128]{2,1,0:T(1,128)}, u32[]{:S(2)}) copy-start(s32[1,1,128]{2,1,0:T(1,128)} %param.13) | copy-start | bytes 1540
  3.0 33.4 %all-to-all-start = ((bf16[8,1024,128]{2,1,0:T(8,128)(2,1)}), bf16[8,1024,128]{2,1,0:T(8,128)(2,1)S(1)}, u32[]{:S(2)}, u32[]{:S(2)}) async-start(bf16[8,1024,128]{2,1,0:T(8,128)(2,1)} %copies.1), calls=%async_computation | async-start | bytes 4194304 | tf_op jit(solution)/shard_map/all_to_all | solution.py:367
  40.9 5.2 %collective-permute-start = (bf16[8,1024,128]{2,1,0:T(8,128)(2,1)S(1)}, bf16[8,1024,128]{2,1,0:T(8,128)(2,1)S(1)}, u32[]{:S(2)}, u32[]{:S(2)}) collective-permute-start(bf16[8,1024,128]{2,1,0:T(8,128)(2,1)S(1)} %forward_tiles.2), channel_id=1, source_target_pairs={{0,8},{8,0},{16,24},{24,16},{32,40},{40,32},{48,56},{56,48},{64,72... | collective-permute-start | bytes 6291464 | tf_op jit(solution)/shard_map/ppermute | solution.py:359
  46.5 35.3 %copy-start = (bf16[1024,128]{1,0:T(8,128)(2,1)S(1)}, bf16[1024,128]{1,0:T(8,128)(2,1)}, u32[]{:S(2)}) copy-start(bf16[1024,128]{1,0:T(8,128)(2,1)} %cot_ref.1) | copy-start | bytes 786436
  46.5 35.3 %copy-start.1 = (bf16[128,128]{1,0:T(8,128)(2,1)S(1)}, bf16[128,128]{1,0:T(8,128)(2,1)}, u32[]{:S(2)}) copy-start(bf16[128,128]{1,0:T(8,128)(2,1)} %weight_ref.1) | copy-start | bytes 98308
  46.6 35.3 %copy-start.4 = (f32[128]{0:T(128)S(1)}, f32[128]{0:T(128)}, u32[]{:S(2)}) copy-start(f32[128]{0:T(128)} %param.10) | copy-start | bytes 1540
  84.9 31.9 %all-to-all-start.2 = ((bf16[8,512,256]{2,1,0:T(8,128)(2,1)}), bf16[8,512,256]{2,1,0:T(8,128)(2,1)S(1)}, u32[]{:S(2)}, u32[]{:S(2)}) async-start(bf16[8,512,256]{2,1,0:T(8,128)(2,1)} %get-tuple-element.17), calls=%async_computation.2 | async-start | bytes 4194304 | tf_op jit(solution)/shard_map/all_to_all | solution.py:363
  88.5 4.4 %collective-permute-start.1 = (f32[136,128]{1,0:T(8,128)S(1)}, f32[136,128]{1,0:T(8,128)S(1)}, u32[]{:S(2)}, u32[]{:S(2)}) collective-permute-start(f32[136,128]{1,0:T(8,128)S(1)} %get-tuple-element.18), channel_id=1, source_target_pairs={{0,2},{1,3},{2,0},{3,1},{4,6},{5,7},{6,4},{7,5},{8,10},{9,11},{10,... | collective-permute-start | bytes 208904 | tf_op jit(solution)/shard_map/ppermute | solution.py:371
  92.9 5.9 %collective-permute-start.2 = (f32[136,128]{1,0:T(8,128)S(1)}, f32[136,128]{1,0:T(8,128)S(1)}, u32[]{:S(2)}, u32[]{:S(2)}) collective-permute-start(f32[136,128]{1,0:T(8,128)S(1)} %add.24), channel_id=1, source_target_pairs={{0,4},{1,5},{2,6},{3,7},{4,0},{5,1},{6,2},{7,3},{8,12},{9,13},{10,... | collective-permute-start | bytes 208904 | tf_op jit(solution)/shard_map/ppermute | solution.py:371
  98.8 1.3 collective-permute-start.3
  100.1 14.6 %collective-permute-start.5 = (f32[136,128]{1,0:T(8,128)S(1)}, f32[136,128]{1,0:T(8,128)S(1)}, u32[]{:S(2)}, u32[]{:S(2)}) collective-permute-start(f32[136,128]{1,0:T(8,128)S(1)} %add.26), channel_id=1, source_target_pairs={{0,16},{8,24},{16,0},{24,8},{32,48},{40,56},{48,32},{56,40},{64,80... | collective-permute-start | bytes 208904 | tf_op jit(solution)/shard_map/ppermute | solution.py:371
  103.6 12.4 %collective-permute-start.6 = (f32[136,128]{1,0:T(8,128)S(1)}, f32[136,128]{1,0:T(8,128)S(1)}, u32[]{:S(2)}, u32[]{:S(2)}) collective-permute-start(f32[136,128]{1,0:T(8,128)S(1)} %add.26), channel_id=1, source_target_pairs={{0,17},{1,16},{2,19},{3,18},{4,21},{5,20},{6,23},{7,22},{8,25},{9,... | collective-permute-start | bytes 208904 | tf_op jit(solution)/shard_map/ppermute | solution.py:394
  103.6 12.4 %collective-permute-start.4 = (f32[136,128]{1,0:T(8,128)S(1)}, f32[136,128]{1,0:T(8,128)S(1)}, u32[]{:S(2)}, u32[]{:S(2)}) collective-permute-start(f32[136,128]{1,0:T(8,128)S(1)} %add.26), channel_id=1, source_target_pairs={{0,1},{1,0},{2,3},{3,2},{4,5},{5,4},{6,7},{7,6},{8,9},{9,8},{10,11... | collective-permute-start | bytes 208904 | tf_op jit(solution)/shard_map/ppermute | solution.py:371
  116.8 4.5 %collective-permute-start.7 = (bf16[8,512,256]{2,1,0:T(8,128)(2,1)S(1)}, bf16[8,512,256]{2,1,0:T(8,128)(2,1)S(1)}, u32[]{:S(2)}, u32[]{:S(2)}) collective-permute-start(bf16[8,512,256]{2,1,0:T(8,128)(2,1)S(1)} %all-to-all-done.2.g), channel_id=1, source_target_pairs={{0,8},{8,0},{16,24},{24,16},{32,40},{40,32},{48,56},{56,48},{64,72... | collective-permute-start | bytes 6291464 | tf_op jit(solution)/shard_map/ppermute | solution.py:359
  126.6 29.9 %all-to-all-start.3 = ((bf16[8,512,256]{2,1,0:T(8,128)(2,1)}), bf16[8,512,256]{2,1,0:T(8,128)(2,1)S(1)}, u32[]{:S(2)}, u32[]{:S(2)}) async-start(bf16[8,512,256]{2,1,0:T(8,128)(2,1)} %backward_tiles.3), calls=%async_computation.3 | async-start | bytes 4194304 | tf_op jit(solution)/shard_map/all_to_all | solution.py:367
  131.1 4.3 %collective-permute-start.8 = (f32[136,128]{1,0:T(8,128)S(1)}, f32[136,128]{1,0:T(8,128)S(1)}, u32[]{:S(2)}, u32[]{:S(2)}) collective-permute-start(f32[136,128]{1,0:T(8,128)S(1)} %add_add_fusion), channel_id=1, source_target_pairs={{0,32},{8,40},{16,48},{24,56},{32,0},{40,8},{48,16},{56,24},{64,96... | collective-permute-start | bytes 208904 | tf_op jit(solution)/shard_map/ppermute | solution.py:371
  135.4 5.9 %collective-permute-start.9 = (f32[136,128]{1,0:T(8,128)S(1)}, f32[136,128]{1,0:T(8,128)S(1)}, u32[]{:S(2)}, u32[]{:S(2)}) collective-permute-start(f32[136,128]{1,0:T(8,128)S(1)} %add.30), channel_id=1, source_target_pairs={{0,64},{8,72},{16,80},{24,88},{32,96},{40,104},{48,112},{56,120},{... | collective-permute-start | bytes 208904 | tf_op jit(solution)/shard_map/ppermute | solution.py:371

commit v4 on v3

--- a/solution.py
+++ b/solution.py
@@ -386,8 +386,8 @@
     hidden, grad, total = dense(recv, weight, bias, cotangent)
 
     grads = row_exchange(grad)
-    for bit in (2, 4):
-        total = total + partner(total, "col", 8, bit)
+    one, two, three = (partner(total, "col", 8, bit) for bit in (2, 4, 6))
+    total = (total + one) + (two + three)
     total = total + partner(total, "row", 16, 1)
     both = [(r * 8 + c, (r ^ 2) * 8 + (c ^ 1)) for r in range(16) for c in range(8)]
     near, far = partner(total, "col", 8, 1), partner(total, "row", 16, 2)

time: 159 us -> 160 us (level)
  the two profiles are of different devices: /device:TPU:0 before, /device:TPU:1 now
where the time goes in v4:
time: 160 us
  waiting for transfers between devices  67.5 us (42%)
  starting transfers between devices  35.2 us (22%)
  blocking collectives  32.8 us (20%)
  Pallas kernels  21.4 us (13%)
    all_to_all x2, waiting for transfers between devices, col_exchange(): return lax.all_to_all(value, 'col', 0, 0)  38.4 us
    all_to_all x1, blocking collectives, row_exchange(): return lax.all_to_all(value, 'row', 0, 0, axis_index_groups=SAME_CORE)  32.8 us
    ppermute x8, waiting for transfers between devices, partner(): return lax.ppermute(value, axis, [(i, i ^ bit) for i in range(size)])  25.9 us
    all_to_all x2, starting transfers between devices, col_exchange(): return lax.all_to_all(value, 'col', 0, 0)  17.5 us
    ppermute x8, starting transfers between devices, partner(): return lax.ppermute(value, axis, [(i, i ^ bit) for i in range(size)])  10.6 us
    pallas_call x2, Pallas kernels, backward(): pl.pallas_call(functools.partial(backward_kernel, which), out_shape=jax.S...  6.39 us
    pallas_call x2, Pallas kernels, forward(): pl.pallas_call(functools.partial(forward_kernel, which), out_shape=jax.Sh...  5.76 us
    all_to_all x1, starting transfers between devices, row_exchange(): return lax.all_to_all(value, 'row', 0, 0, axis_index_groups=SAME_CORE)  3.61 us
  transfers between devices with their start and end apart: 14, of which 11 were waited for; matrix products, arithmetic and copies ran while one was open for 1% of the time, Pallas kernels for 5%

profile of v4, /device:TPU:1, one launch (start us, length us, event | category | flops | bytes accessed | tf_op | source)
XLA Modules:
  0.0 159.6 jit_solution(10154487742005392336)
XLA Ops:
  0.6 2.4 %copies.1 = bf16[8,1024,128]{2,1,0:T(8,128)(2,1)} custom-call(bf16[1024,128]{1,0:T(8,128)(2,1)} %value_ref.1), custom_call_target="tpu_custom_call" | custom-call | tf_op jit(solution)/shard_map/copies/pallas_call | solution.py:94
  3.0 0.0 copy-start.2
  3.0 0.0 copy-start.3
  3.0 6.9 %all-to-all-start = ((bf16[8,1024,128]{2,1,0:T(8,128)(2,1)}), bf16[8,1024,128]{2,1,0:T(8,128)(2,1)S(1)}, u32[]{:S(2)}, u32[]{:S(2)}) async-start(bf16[8,1024,128]{2,1,0:T(8,128)(2,1)} %copies.1), calls=%async_computation | async-start | bytes 4194304 | tf_op jit(solution)/shard_map/all_to_all | solution.py:367
  10.6 0.0 copy-done.2
  10.6 0.0 copy-done.3
  10.6 2.3 %slot_lists.1.lists_ref = s32[1024]{0:T(1024)S(4)} custom-call(s32[1]{0:T(128)} %bitcast.where_ref, s32[128]{0:T(128)S(1)} %bitcast.9, s32[128]{0:T(128)S(1)} %bitcast.10, s32[1]{0:T(128)} %bitcast.8.count_ref), custom_call_target="tpu_custom_call" | custom-call | tf_op jit(solution)/shard_map/slot_lists/pallas_call | solution.py:72
  12.9 23.1 %all-to-all-done.x = bf16[8,1024,128]{2,1,0:T(8,128)(2,1)S(1)} async-done(((bf16[8,1024,128]{2,1,0:T(8,128)(2,1)}), bf16[8,1024,128]{2,1,0:T(8,128)(2,1)S(1)}, u32[]{:S(2)}, u32[]{:S(2)}) %all-to-all-start) | async-done | bytes 2097184 | tf_op jit(solution)/shard_map/all_to_all | solution.py:367
  36.0 2.7 %forward_tiles.2 = bf16[8,1024,128]{2,1,0:T(8,128)(2,1)S(1)} custom-call(s32[1024]{0:T(1024)S(4)} %slot_lists.1.lists_ref, bf16[128,256,256]{2,1,0:T(8,128)(2,1)} %bitcast.12, bf16[8,1024,128]{2,1,0:T(8,128)(2,1)S(1)} %all-to-all-done.x), custom_call_target="tpu_custom_call" | custom-call | flops 1073741824 | bytes 16777216 | tf_op jit(solution)/shard_map/forward_tiles/pallas_call | solution.py:181
  38.6 2.1 %collective-permute-start = (bf16[8,1024,128]{2,1,0:T(8,128)(2,1)S(1)}, bf16[8,1024,128]{2,1,0:T(8,128)(2,1)S(1)}, u32[]{:S(2)}, u32[]{:S(2)}) collective-permute-start(bf16[8,1024,128]{2,1,0:T(8,128)(2,1)S(1)} %forward_tiles.2), channel_id=1, source_target_pairs={{0,8},{8,0},{16,24},{24,16},{32,40},{40,32},{48,56},{56,48},{64,72... | collective-permute-start | bytes 6291464 | tf_op jit(solution)/shard_map/ppermute | solution.py:359
  40.8 3.1 %forward_tiles.3.mine_ref = bf16[8,1024,128]{2,1,0:T(8,128)(2,1)S(1)} custom-call(s32[1024]{0:T(1024)S(4)} %slot_lists.1.lists_ref, bf16[128,256,256]{2,1,0:T(8,128)(2,1)} %bitcast.13, bf16[8,1024,128]{2,1,0:T(8,128)(2,1)S(1)} %all-to-all-done.x), custom_call_target="tpu_custom_call" | custom-call | flops 1073741824 | bytes 16777216 | tf_op jit(solution)/shard_map/forward_tiles/pallas_call | solution.py:181
  43.9 0.7 collective-permute-done.other_ref
  44.6 0.5 pair_sum.1
  45.0 0.0 copy-start
  45.1 0.0 copy-start.1
  45.1 0.0 copy-start.4
  45.1 32.8 %all_to_all.20.recv_ref = bf16[8,1024,128]{2,1,0:T(8,128)(2,1)S(1)} all-to-all(bf16[8,1024,128]{2,1,0:T(8,128)(2,1)S(1)} %pair_sum.1), channel_id=1, replica_groups={{0,16,32,48,64,80,96,112},{8,24,40,56,72,88,104,120},{1,17,33,49,65,81,..., dimensions={0} | all-to-all | bytes 4194304 | tf_op jit(solution)/shard_map/all_to_all | solution.py:363
  77.9 0.0 copy-done
  77.9 0.0 copy-done.1
  77.9 0.0 copy-done.4
  77.9 3.0 %dense_layer.1 = (bf16[1024,128]{1,0:T(8,128)(2,1)}, bf16[8,512,256]{2,1,0:T(8,128)(2,1)}, f32[136,128]{1,0:T(8,128)S(1)}) custom-call(bf16[8,1024,128]{2,1,0:T(8,128)(2,1)S(1)} %all_to_all.20.recv_ref, bf16[128,128]{1,0:T(8,128)(2,1)S(1)} %copy-done.1, f32[1,128]{1,0:T(1,128)S(1)} %bitcast.11, bf16[1024,128]{1,0:T(8,128)(2,1)S(1)} %copy-done), custom_call_target="tpu_custom_call" | custom-call | flops 100663296 | bytes 5242880 | tf_op jit(solution)/shard_map/dense_layer/pallas_call | solution.py:312
  80.9 3.6 %all-to-all-start.2 = ((bf16[8,512,256]{2,1,0:T(8,128)(2,1)}), bf16[8,512,256]{2,1,0:T(8,128)(2,1)S(1)}, u32[]{:S(2)}, u32[]{:S(2)}) async-start(bf16[8,512,256]{2,1,0:T(8,128)(2,1)} %get-tuple-element.17), calls=%async_computation.2 | async-start | bytes 4194304 | tf_op jit(solution)/shard_map/all_to_all | solution.py:363
  84.5 3.6 %collective-permute-start.2 = (f32[136,128]{1,0:T(8,128)S(1)}, f32[136,128]{1,0:T(8,128)S(1)}, u32[]{:S(2)}, u32[]{:S(2)}) collective-permute-start(f32[136,128]{1,0:T(8,128)S(1)} %get-tuple-element.18), channel_id=1, source_target_pairs={{0,4},{1,5},{2,6},{3,7},{4,0},{5,1},{6,2},{7,3},{8,12},{9,13},{10,... | collective-permute-start | bytes 208904 | tf_op jit(solution)/shard_map/ppermute | solution.py:371
  88.2 0.0 collective-permute-start.3
  88.2 0.0 collective-permute-start.1
  88.2 1.7 %collective-permute-done.2 = f32[136,128]{1,0:T(8,128)S(1)} collective-permute-done((f32[136,128]{1,0:T(8,128)S(1)}, f32[136,128]{1,0:T(8,128)S(1)}, u32[]{:S(2)}, u32[]{:S(2)}) %collective-permute-start.2) | collective-permute-done | bytes 69664 | tf_op jit(solution)/shard_map/ppermute | solution.py:371
  89.9 3.3 %collective-permute-done.3 = f32[136,128]{1,0:T(8,128)S(1)} collective-permute-done((f32[136,128]{1,0:T(8,128)S(1)}, f32[136,128]{1,0:T(8,128)S(1)}, u32[]{:S(2)}, u32[]{:S(2)}) %collective-permute-start.3) | collective-permute-done | bytes 69664 | tf_op jit(solution)/shard_map/ppermute | solution.py:371
  93.1 0.0 collective-permute-done.1
  93.2 3.3 %collective-permute-start.4 = (f32[136,128]{1,0:T(8,128)S(1)}, f32[136,128]{1,0:T(8,128)S(1)}, u32[]{:S(2)}, u32[]{:S(2)}) collective-permute-start(f32[136,128]{1,0:T(8,128)S(1)} %add_add_fusion.1), channel_id=1, source_target_pairs={{0,8},{8,0},{16,24},{24,16},{32,40},{40,32},{48,56},{56,48},{64,72... | collective-permute-start | bytes 208904 | tf_op jit(solution)/shard_map/ppermute | solution.py:371
  96.4 0.9 collective-permute-done.4
  97.3 3.1 %collective-permute-start.6 = (f32[136,128]{1,0:T(8,128)S(1)}, f32[136,128]{1,0:T(8,128)S(1)}, u32[]{:S(2)}, u32[]{:S(2)}) collective-permute-start(f32[136,128]{1,0:T(8,128)S(1)} %add.30), channel_id=1, source_target_pairs={{0,16},{8,24},{16,0},{24,8},{32,48},{40,56},{48,32},{56,40},{64,80... | collective-permute-start | bytes 208904 | tf_op jit(solution)/shard_map/ppermute | solution.py:371
  100.5 0.1 collective-permute-start.7
  100.6 0.5 collective-permute-start.5
  101.1 11.6 %collective-permute-done.6 = f32[136,128]{1,0:T(8,128)S(1)} collective-permute-done((f32[136,128]{1,0:T(8,128)S(1)}, f32[136,128]{1,0:T(8,128)S(1)}, u32[]{:S(2)}, u32[]{:S(2)}) %collective-permute-start.6) | collective-permute-done | bytes 69664 | tf_op jit(solution)/shard_map/ppermute | solution.py:371
  112.7 1.5 collective-permute-done.7
  114.2 0.0 collective-permute-done.5
  114.2 0.0 all-to-all-done.2.g
  114.2 1.3 collective-permute-start.8
  115.5 2.7 %backward_tiles.2.rest_0_ = bf16[8,512,256]{2,1,0:T(8,128)(2,1)S(1)} custom-call(s32[1024]{0:T(1024)S(4)} %slot_lists.1.lists_ref, bf16[128,256,256]{2,1,0:T(8,128)(2,1)} %bitcast.14, bf16[8,512,256]{2,1,0:T(8,128)(2,1)S(1)} %all-to-all-done.2.g), custom_call_target="tpu_custom_call" | custom-call | flops 1073741824 | bytes 16777216 | tf_op jit(solution)/shard_map/backward_tiles/pallas_call | solution.py:258
  118.3 1.0 collective-permute-done.8.g
  119.3 3.6 %backward_tiles.3 = bf16[8,512,256]{2,1,0:T(8,128)(2,1)} custom-call(s32[1024]{0:T(1024)S(4)} %slot_lists.1.lists_ref, bf16[128,256,256]{2,1,0:T(8,128)(2,1)} %bitcast.15, bf16[8,512,256]{2,1,0:T(8,128)(2,1)S(1)} %collective-permute-done.8.g, bf16[8,512,256]{2,1,0:T(8,128)(2,1)S(1)} %backward_tiles.2.rest_0_), custom_call_target="tpu_custom_call" | custom-call | flops 1073741824 | bytes 16777216 | tf_op jit(solution)/shard_map/backward_tiles/pallas_call | solution.py:258
  123.0 10.6 %all-to-all-start.3 = ((bf16[8,512,256]{2,1,0:T(8,128)(2,1)}), bf16[8,512,256]{2,1,0:T(8,128)(2,1)S(1)}, u32[]{:S(2)}, u32[]{:S(2)}) async-start(bf16[8,512,256]{2,1,0:T(8,128)(2,1)} %backward_tiles.3), calls=%async_computation.3 | async-start | bytes 4194304 | tf_op jit(solution)/shard_map/all_to_all | solution.py:367
  133.6 0.0 collective-permute-start.9
  133.6 3.4 %collective-permute-done.9 = f32[136,128]{1,0:T(8,128)S(1)} collective-permute-done((f32[136,128]{1,0:T(8,128)S(1)}, f32[136,128]{1,0:T(8,128)S(1)}, u32[]{:S(2)}, u32[]{:S(2)}) %collective-permute-start.9) | collective-permute-done | bytes 69664 | tf_op jit(solution)/shard_map/ppermute | solution.py:371
  137.0 0.1 collective-permute-start.10
  137.1 4.9 %collective-permute-done.10 = f32[136,128]{1,0:T(8,128)S(1)} collective-permute-done((f32[136,128]{1,0:T(8,128)S(1)}, f32[136,128]{1,0:T(8,128)S(1)}, u32[]{:S(2)}, u32[]{:S(2)}) %collective-permute-start.10) | collective-permute-done | bytes 69664 | tf_op jit(solution)/shard_map/ppermute | solution.py:371
  142.1 0.5 fusion
  142.6 0.6 slice_multiply_fusion
  143.2 15.3 %all-to-all-done.3.recv_ref = bf16[8,512,256]{2,1,0:T(8,128)(2,1)S(1)} async-done(((bf16[8,512,256]{2,1,0:T(8,128)(2,1)}), bf16[8,512,256]{2,1,0:T(8,128)(2,1)S(1)}, u32[]{:S(2)}, u32[]{:S(2)}) %all-to-all-start.3) | async-done | bytes 2097184 | tf_op jit(solution)/shard_map/all_to_all | solution.py:367
  158.5 1.0 last_sum.1
  (5 shorter events, 0.1 us)
Async XLA Ops:
  3.0 7.6 %copy-start.2 = (s32[1,1,128]{2,1,0:T(1,128)S(1)}, s32[1,1,128]{2,1,0:T(1,128)}, u32[]{:S(2)}) copy-start(s32[1,1,128]{2,1,0:T(1,128)} %param.12) | copy-start | bytes 1540
  3.0 7.6 %copy-start.3 = (s32[1,1,128]{2,1,0:T(1,128)S(1)}, s32[1,1,128]{2,1,0:T(1,128)}, u32[]{:S(2)}) copy-start(s32[1,1,128]{2,1,0:T(1,128)} %param.13) | copy-start | bytes 1540
  3.0 33.0 %all-to-all-start = ((bf16[8,1024,128]{2,1,0:T(8,128)(2,1)}), bf16[8,1024,128]{2,1,0:T(8,128)(2,1)S(1)}, u32[]{:S(2)}, u32[]{:S(2)}) async-start(bf16[8,1024,128]{2,1,0:T(8,128)(2,1)} %copies.1), calls=%async_computation | async-start | bytes 4194304 | tf_op jit(solution)/shard_map/all_to_all | solution.py:367
  38.6 5.9 %collective-permute-start = (bf16[8,1024,128]{2,1,0:T(8,128)(2,1)S(1)}, bf16[8,1024,128]{2,1,0:T(8,128)(2,1)S(1)}, u32[]{:S(2)}, u32[]{:S(2)}) collective-permute-start(bf16[8,1024,128]{2,1,0:T(8,128)(2,1)S(1)} %forward_tiles.2), channel_id=1, source_target_pairs={{0,8},{8,0},{16,24},{24,16},{32,40},{40,32},{48,56},{56,48},{64,72... | collective-permute-start | bytes 6291464 | tf_op jit(solution)/shard_map/ppermute | solution.py:359
  45.0 32.8 %copy-start = (bf16[1024,128]{1,0:T(8,128)(2,1)S(1)}, bf16[1024,128]{1,0:T(8,128)(2,1)}, u32[]{:S(2)}) copy-start(bf16[1024,128]{1,0:T(8,128)(2,1)} %cot_ref.1) | copy-start | bytes 786436
  45.1 32.8 %copy-start.1 = (bf16[128,128]{1,0:T(8,128)(2,1)S(1)}, bf16[128,128]{1,0:T(8,128)(2,1)}, u32[]{:S(2)}) copy-start(bf16[128,128]{1,0:T(8,128)(2,1)} %weight_ref.1) | copy-start | bytes 98308
  45.1 32.8 %copy-start.4 = (f32[128]{0:T(128)S(1)}, f32[128]{0:T(128)}, u32[]{:S(2)}) copy-start(f32[128]{0:T(128)} %param.10) | copy-start | bytes 1540
  80.9 33.3 %all-to-all-start.2 = ((bf16[8,512,256]{2,1,0:T(8,128)(2,1)}), bf16[8,512,256]{2,1,0:T(8,128)(2,1)S(1)}, u32[]{:S(2)}, u32[]{:S(2)}) async-start(bf16[8,512,256]{2,1,0:T(8,128)(2,1)} %get-tuple-element.17), calls=%async_computation.2 | async-start | bytes 4194304 | tf_op jit(solution)/shard_map/all_to_all | solution.py:363
  84.5 5.3 %collective-permute-start.2 = (f32[136,128]{1,0:T(8,128)S(1)}, f32[136,128]{1,0:T(8,128)S(1)}, u32[]{:S(2)}, u32[]{:S(2)}) collective-permute-start(f32[136,128]{1,0:T(8,128)S(1)} %get-tuple-element.18), channel_id=1, source_target_pairs={{0,4},{1,5},{2,6},{3,7},{4,0},{5,1},{6,2},{7,3},{8,12},{9,13},{10,... | collective-permute-start | bytes 208904 | tf_op jit(solution)/shard_map/ppermute | solution.py:371
  88.2 5.0 %collective-permute-start.3 = (f32[136,128]{1,0:T(8,128)S(1)}, f32[136,128]{1,0:T(8,128)S(1)}, u32[]{:S(2)}, u32[]{:S(2)}) collective-permute-start(f32[136,128]{1,0:T(8,128)S(1)} %get-tuple-element.18), channel_id=1, source_target_pairs={{0,6},{1,7},{2,4},{3,5},{4,2},{5,3},{6,0},{7,1},{8,14},{9,15},{10,... | collective-permute-start | bytes 208904 | tf_op jit(solution)/shard_map/ppermute | solution.py:371
  88.2 5.0 %collective-permute-start.1 = (f32[136,128]{1,0:T(8,128)S(1)}, f32[136,128]{1,0:T(8,128)S(1)}, u32[]{:S(2)}, u32[]{:S(2)}) collective-permute-start(f32[136,128]{1,0:T(8,128)S(1)} %get-tuple-element.18), channel_id=1, source_target_pairs={{0,2},{1,3},{2,0},{3,1},{4,6},{5,7},{6,4},{7,5},{8,10},{9,11},{10,... | collective-permute-start | bytes 208904 | tf_op jit(solution)/shard_map/ppermute | solution.py:371
  93.2 4.2 %collective-permute-start.4 = (f32[136,128]{1,0:T(8,128)S(1)}, f32[136,128]{1,0:T(8,128)S(1)}, u32[]{:S(2)}, u32[]{:S(2)}) collective-permute-start(f32[136,128]{1,0:T(8,128)S(1)} %add_add_fusion.1), channel_id=1, source_target_pairs={{0,8},{8,0},{16,24},{24,16},{32,40},{40,32},{48,56},{56,48},{64,72... | collective-permute-start | bytes 208904 | tf_op jit(solution)/shard_map/ppermute | solution.py:371
  97.3 15.3 %collective-permute-start.6 = (f32[136,128]{1,0:T(8,128)S(1)}, f32[136,128]{1,0:T(8,128)S(1)}, u32[]{:S(2)}, u32[]{:S(2)}) collective-permute-start(f32[136,128]{1,0:T(8,128)S(1)} %add.30), channel_id=1, source_target_pairs={{0,16},{8,24},{16,0},{24,8},{32,48},{40,56},{48,32},{56,40},{64,80... | collective-permute-start | bytes 208904 | tf_op jit(solution)/shard_map/ppermute | solution.py:371
  100.5 13.7 %collective-permute-start.7 = (f32[136,128]{1,0:T(8,128)S(1)}, f32[136,128]{1,0:T(8,128)S(1)}, u32[]{:S(2)}, u32[]{:S(2)}) collective-permute-start(f32[136,128]{1,0:T(8,128)S(1)} %add.30), channel_id=1, source_target_pairs={{0,17},{1,16},{2,19},{3,18},{4,21},{5,20},{6,23},{7,22},{8,25},{9,... | collective-permute-start | bytes 208904 | tf_op jit(solution)/shard_map/ppermute | solution.py:394
  100.6 13.6 %collective-permute-start.5 = (f32[136,128]{1,0:T(8,128)S(1)}, f32[136,128]{1,0:T(8,128)S(1)}, u32[]{:S(2)}, u32[]{:S(2)}) collective-permute-start(f32[136,128]{1,0:T(8,128)S(1)} %add.30), channel_id=1, source_target_pairs={{0,1},{1,0},{2,3},{3,2},{4,5},{5,4},{6,7},{7,6},{8,9},{9,8},{10,11... | collective-permute-start | bytes 208904 | tf_op jit(solution)/shard_map/ppermute | solution.py:371
  114.2 5.0 %collective-permute-start.8 = (bf16[8,512,256]{2,1,0:T(8,128)(2,1)S(1)}, bf16[8,512,256]{2,1,0:T(8,128)(2,1)S(1)}, u32[]{:S(2)}, u32[]{:S(2)}) collective-permute-start(bf16[8,512,256]{2,1,0:T(8,128)(2,1)S(1)} %all-to-all-done.2.g), channel_id=1, source_target_pairs={{0,8},{8,0},{16,24},{24,16},{32,40},{40,32},{48,56},{56,48},{64,72... | collective-permute-start | bytes 6291464 | tf_op jit(solution)/shard_map/ppermute | solution.py:359
  123.0 35.6 %all-to-all-start.3 = ((bf16[8,512,256]{2,1,0:T(8,128)(2,1)}), bf16[8,512,256]{2,1,0:T(8,128)(2,1)S(1)}, u32[]{:S(2)}, u32[]{:S(2)}) async-start(bf16[8,512,256]{2,1,0:T(8,128)(2,1)} %backward_tiles.3), calls=%async_computation.3 | async-start | bytes 4194304 | tf_op jit(solution)/shard_map/all_to_all | solution.py:367
  133.6 3.5 %collective-permute-start.9 = (f32[136,128]{1,0:T(8,128)S(1)}, f32[136,128]{1,0:T(8,128)S(1)}, u32[]{:S(2)}, u32[]{:S(2)}) collective-permute-start(f32[136,128]{1,0:T(8,128)S(1)} %add_add_fusion), channel_id=1, source_target_pairs={{0,32},{8,40},{16,48},{24,56},{32,0},{40,8},{48,16},{56,24},{64,96... | collective-permute-start | bytes 208904 | tf_op jit(solution)/shard_map/ppermute | solution.py:371
  137.0 5.0 %collective-permute-start.10 = (f32[136,128]{1,0:T(8,128)S(1)}, f32[136,128]{1,0:T(8,128)S(1)}, u32[]{:S(2)}, u32[]{:S(2)}) collective-permute-start(f32[136,128]{1,0:T(8,128)S(1)} %add.34), channel_id=1, source_target_pairs={{0,64},{8,72},{16,80},{24,88},{32,96},{40,104},{48,112},{56,120},{... | collective-permute-start | bytes 208904 | tf_op jit(solution)/shard_map/ppermute | solution.py:371

commit v5 on v4

--- a/solution.py
+++ b/solution.py
@@ -392,7 +392,6 @@
     both = [(r * 8 + c, (r ^ 2) * 8 + (c ^ 1)) for r in range(16) for c in range(8)]
     near, far = partner(total, "col", 8, 1), partner(total, "row", 16, 2)
     total = (total + near) + (far + lax.ppermute(total, ("row", "col"), both))
-    grads, total = order((grads, total))
     other = to_other_core(grads)
     back = backward(2, lists, values, grads)
     back = backward(3, lists, values, other, back)

time: 160 us -> 181 us (1.13)
  the two profiles are of different devices: /device:TPU:1 before, /device:TPU:0 now
where the time goes in v5:
time: 181 us
  waiting for transfers between devices  68.6 us (38%)
  blocking collectives  66.2 us (37%)
  starting transfers between devices  23.8 us (13%)
  Pallas kernels  19.8 us (11%)
    all_to_all x2, blocking collectives, row_exchange(): return lax.all_to_all(value, 'row', 0, 0, axis_index_groups=SAME_CORE)  66.2 us
    ppermute x8, waiting for transfers between devices, partner(): return lax.ppermute(value, axis, [(i, i ^ bit) for i in range(size)])  39.1 us
    all_to_all x2, waiting for transfers between devices, col_exchange(): return lax.all_to_all(value, 'col', 0, 0)  24.3 us
    all_to_all x2, starting transfers between devices, col_exchange(): return lax.all_to_all(value, 'col', 0, 0)  13.8 us
    pallas_call x2, Pallas kernels, backward(): pl.pallas_call(functools.partial(backward_kernel, which), out_shape=jax.S...  5.83 us
    ppermute x8, starting transfers between devices, partner(): return lax.ppermute(value, axis, [(i, i ^ bit) for i in range(size)])  5.77 us
    pallas_call x2, Pallas kernels, forward(): pl.pallas_call(functools.partial(forward_kernel, which), out_shape=jax.Sh...  4.9 us
    ppermute x1, starting transfers between devices, local(): total = total + near + (far + lax.ppermute(total, ('row', 'col'), both))  4.12 us
  transfers between devices with their start and end apart: 13, of which 11 were waited for; matrix products, arithmetic and copies ran while one was open for 1% of the time, Pallas kernels for 4%

profile of v5, /device:TPU:0, one launch (start us, length us, event | category | flops | bytes accessed | tf_op | source)
XLA Modules:
  0.0 181.1 jit_solution(7922122542910675408)
XLA Ops:
  0.6 2.4 %copies.1 = bf16[8,1024,128]{2,1,0:T(8,128)(2,1)} custom-call(bf16[1024,128]{1,0:T(8,128)(2,1)} %value_ref.1), custom_call_target="tpu_custom_call" | custom-call | tf_op jit(solution)/shard_map/copies/pallas_call | solution.py:94
  3.0 0.0 copy-start.2
  3.0 0.0 copy-start.3
  3.0 6.4 %all-to-all-start = ((bf16[8,1024,128]{2,1,0:T(8,128)(2,1)}), bf16[8,1024,128]{2,1,0:T(8,128)(2,1)S(1)}, u32[]{:S(2)}, u32[]{:S(2)}) async-start(bf16[8,1024,128]{2,1,0:T(8,128)(2,1)} %copies.1), calls=%async_computation | async-start | bytes 4194304 | tf_op jit(solution)/shard_map/all_to_all | solution.py:367
  10.1 0.0 copy-done.2
  10.1 0.0 copy-done.3
  10.1 2.0 %slot_lists.1.lists_ref = s32[1024]{0:T(1024)S(4)} custom-call(s32[1]{0:T(128)} %bitcast.where_ref, s32[128]{0:T(128)S(1)} %bitcast.9, s32[128]{0:T(128)S(1)} %bitcast.10, s32[1]{0:T(128)} %bitcast.8.count_ref), custom_call_target="tpu_custom_call" | custom-call | tf_op jit(solution)/shard_map/slot_lists/pallas_call | solution.py:72
  12.2 24.3 %all-to-all-done.x = bf16[8,1024,128]{2,1,0:T(8,128)(2,1)S(1)} async-done(((bf16[8,1024,128]{2,1,0:T(8,128)(2,1)}), bf16[8,1024,128]{2,1,0:T(8,128)(2,1)S(1)}, u32[]{:S(2)}, u32[]{:S(2)}) %all-to-all-start) | async-done | bytes 2097184 | tf_op jit(solution)/shard_map/all_to_all | solution.py:367
  36.4 2.7 %forward_tiles.2 = bf16[8,1024,128]{2,1,0:T(8,128)(2,1)S(1)} custom-call(s32[1024]{0:T(1024)S(4)} %slot_lists.1.lists_ref, bf16[128,256,256]{2,1,0:T(8,128)(2,1)} %bitcast.12, bf16[8,1024,128]{2,1,0:T(8,128)(2,1)S(1)} %all-to-all-done.x), custom_call_target="tpu_custom_call" | custom-call | flops 1073741824 | bytes 16777216 | tf_op jit(solution)/shard_map/forward_tiles/pallas_call | solution.py:181
  39.1 0.1 collective-permute-start
  39.2 2.2 %forward_tiles.3.mine_ref = bf16[8,1024,128]{2,1,0:T(8,128)(2,1)S(1)} custom-call(s32[1024]{0:T(1024)S(4)} %slot_lists.1.lists_ref, bf16[128,256,256]{2,1,0:T(8,128)(2,1)} %bitcast.13, bf16[8,1024,128]{2,1,0:T(8,128)(2,1)S(1)} %all-to-all-done.x), custom_call_target="tpu_custom_call" | custom-call | flops 1073741824 | bytes 16777216 | tf_op jit(solution)/shard_map/forward_tiles/pallas_call | solution.py:181
  41.4 1.9 %collective-permute-done.other_ref = bf16[8,1024,128]{2,1,0:T(8,128)(2,1)S(1)} collective-permute-done((bf16[8,1024,128]{2,1,0:T(8,128)(2,1)S(1)}, bf16[8,1024,128]{2,1,0:T(8,128)(2,1)S(1)}, u32[]{:S(2)}, u32[]{:S(2)}) %collective-permute-start) | collective-permute-done | bytes 2097184 | tf_op jit(solution)/shard_map/ppermute | solution.py:359
  43.3 0.5 pair_sum.1
  43.8 0.0 copy-start
  43.8 0.0 copy-start.1
  43.8 0.0 copy-start.4
  43.8 35.5 %all_to_all.20.recv_ref = bf16[8,1024,128]{2,1,0:T(8,128)(2,1)S(1)} all-to-all(bf16[8,1024,128]{2,1,0:T(8,128)(2,1)S(1)} %pair_sum.1), channel_id=1, replica_groups={{0,16,32,48,64,80,96,112},{8,24,40,56,72,88,104,120},{1,17,33,49,65,81,..., dimensions={0} | all-to-all | bytes 4194304 | tf_op jit(solution)/shard_map/all_to_all | solution.py:363
  79.3 0.0 copy-done
  79.4 0.0 copy-done.1
  79.4 0.0 copy-done.4
  79.4 3.1 %dense_layer.1 = (bf16[1024,128]{1,0:T(8,128)(2,1)}, bf16[8,512,256]{2,1,0:T(8,128)(2,1)}, f32[136,128]{1,0:T(8,128)S(1)}) custom-call(bf16[8,1024,128]{2,1,0:T(8,128)(2,1)S(1)} %all_to_all.20.recv_ref, bf16[128,128]{1,0:T(8,128)(2,1)S(1)} %copy-done.1, f32[1,128]{1,0:T(1,128)S(1)} %bitcast.11, bf16[1024,128]{1,0:T(8,128)(2,1)S(1)} %copy-done), custom_call_target="tpu_custom_call" | custom-call | flops 100663296 | bytes 5242880 | tf_op jit(solution)/shard_map/dense_layer/pallas_call | solution.py:312
  82.5 30.7 %all_to_all.21.g = bf16[8,512,256]{2,1,0:T(8,128)(2,1)S(1)} all-to-all(bf16[8,512,256]{2,1,0:T(8,128)(2,1)} %get-tuple-element.15), channel_id=1, replica_groups={{0,16,32,48,64,80,96,112},{8,24,40,56,72,88,104,120},{1,17,33,49,65,81,..., dimensions={0} | all-to-all | bytes 4194304 | tf_op jit(solution)/shard_map/all_to_all | solution.py:363
  113.1 0.0 collective-permute-start.1
  113.1 2.1 %backward_tiles.2.rest_0_ = bf16[8,512,256]{2,1,0:T(8,128)(2,1)S(1)} custom-call(s32[1024]{0:T(1024)S(4)} %slot_lists.1.lists_ref, bf16[128,256,256]{2,1,0:T(8,128)(2,1)} %bitcast.14, bf16[8,512,256]{2,1,0:T(8,128)(2,1)S(1)} %all_to_all.21.g), custom_call_target="tpu_custom_call" | custom-call | flops 1073741824 | bytes 16777216 | tf_op jit(solution)/shard_map/backward_tiles/pallas_call | solution.py:258
  115.2 2.0 %collective-permute-done.1.g = bf16[8,512,256]{2,1,0:T(8,128)(2,1)S(1)} collective-permute-done((bf16[8,512,256]{2,1,0:T(8,128)(2,1)S(1)}, bf16[8,512,256]{2,1,0:T(8,128)(2,1)S(1)}, u32[]{:S(2)}, u32[]{:S(2)}) %collective-permute-start.1) | collective-permute-done | bytes 2097184 | tf_op jit(solution)/shard_map/ppermute | solution.py:359
  117.3 3.7 %backward_tiles.3 = bf16[8,512,256]{2,1,0:T(8,128)(2,1)} custom-call(s32[1024]{0:T(1024)S(4)} %slot_lists.1.lists_ref, bf16[128,256,256]{2,1,0:T(8,128)(2,1)} %bitcast.15, bf16[8,512,256]{2,1,0:T(8,128)(2,1)S(1)} %collective-permute-done.1.g, bf16[8,512,256]{2,1,0:T(8,128)(2,1)S(1)} %backward_tiles.2.rest_0_), custom_call_target="tpu_custom_call" | custom-call | flops 1073741824 | bytes 16777216 | tf_op jit(solution)/shard_map/backward_tiles/pallas_call | solution.py:258
  121.0 7.4 %all-to-all-start.3 = ((bf16[8,512,256]{2,1,0:T(8,128)(2,1)}), bf16[8,512,256]{2,1,0:T(8,128)(2,1)S(1)}, u32[]{:S(2)}, u32[]{:S(2)}) async-start(bf16[8,512,256]{2,1,0:T(8,128)(2,1)} %backward_tiles.3), calls=%async_computation.3 | async-start | bytes 4194304 | tf_op jit(solution)/shard_map/all_to_all | solution.py:367
  128.5 3.5 %collective-permute-start.3 = (f32[136,128]{1,0:T(8,128)S(1)}, f32[136,128]{1,0:T(8,128)S(1)}, u32[]{:S(2)}, u32[]{:S(2)}) collective-permute-start(f32[136,128]{1,0:T(8,128)S(1)} %get-tuple-element.16), channel_id=1, source_target_pairs={{0,4},{1,5},{2,6},{3,7},{4,0},{5,1},{6,2},{7,3},{8,12},{9,13},{10,... | collective-permute-start | bytes 208904 | tf_op jit(solution)/shard_map/ppermute | solution.py:371
  132.0 1.2 collective-permute-start.4
  133.1 0.0 collective-permute-start.2
  133.2 19.4 %collective-permute-done.3 = f32[136,128]{1,0:T(8,128)S(1)} collective-permute-done((f32[136,128]{1,0:T(8,128)S(1)}, f32[136,128]{1,0:T(8,128)S(1)}, u32[]{:S(2)}, u32[]{:S(2)}) %collective-permute-start.3) | collective-permute-done | bytes 69664 | tf_op jit(solution)/shard_map/ppermute | solution.py:371
  152.5 6.1 %collective-permute-done.4 = f32[136,128]{1,0:T(8,128)S(1)} collective-permute-done((f32[136,128]{1,0:T(8,128)S(1)}, f32[136,128]{1,0:T(8,128)S(1)}, u32[]{:S(2)}, u32[]{:S(2)}) %collective-permute-start.4) | collective-permute-done | bytes 69664 | tf_op jit(solution)/shard_map/ppermute | solution.py:371
  158.6 0.0 collective-permute-done.2
  158.7 0.2 collective-permute-start.5
  158.9 1.1 collective-permute-done.5
  160.0 0.1 collective-permute-start.7
  160.1 4.1 %collective-permute-start.8 = (f32[136,128]{1,0:T(8,128)S(1)}, f32[136,128]{1,0:T(8,128)S(1)}, u32[]{:S(2)}, u32[]{:S(2)}) collective-permute-start(f32[136,128]{1,0:T(8,128)S(1)} %add.30), channel_id=1, source_target_pairs={{0,17},{1,16},{2,19},{3,18},{4,21},{5,20},{6,23},{7,22},{8,25},{9,... | collective-permute-start | bytes 208904 | tf_op jit(solution)/shard_map/ppermute | solution.py:394
  164.2 0.0 collective-permute-start.6
  164.2 1.7 collective-permute-done.7
  166.0 1.4 collective-permute-done.8
  167.3 1.2 collective-permute-done.6
  168.6 0.1 collective-permute-start.9
  168.7 4.3 %collective-permute-done.9 = f32[136,128]{1,0:T(8,128)S(1)} collective-permute-done((f32[136,128]{1,0:T(8,128)S(1)}, f32[136,128]{1,0:T(8,128)S(1)}, u32[]{:S(2)}, u32[]{:S(2)}) %collective-permute-start.9) | collective-permute-done | bytes 69664 | tf_op jit(solution)/shard_map/ppermute | solution.py:371
  173.0 0.7 collective-permute-start.10
  173.7 5.2 %collective-permute-done.10 = f32[136,128]{1,0:T(8,128)S(1)} collective-permute-done((f32[136,128]{1,0:T(8,128)S(1)}, f32[136,128]{1,0:T(8,128)S(1)}, u32[]{:S(2)}, u32[]{:S(2)}) %collective-permute-start.10) | collective-permute-done | bytes 69664 | tf_op jit(solution)/shard_map/ppermute | solution.py:371
  178.9 0.5 fusion
  179.4 0.6 slice_multiply_fusion
  180.0 0.0 all-to-all-done.3.recv_ref
  180.0 1.0 last_sum.1
  (5 shorter events, 0.1 us)
Async XLA Ops:
  3.0 7.1 %copy-start.2 = (s32[1,1,128]{2,1,0:T(1,128)S(1)}, s32[1,1,128]{2,1,0:T(1,128)}, u32[]{:S(2)}) copy-start(s32[1,1,128]{2,1,0:T(1,128)} %param.12) | copy-start | bytes 1540
  3.0 7.1 %copy-start.3 = (s32[1,1,128]{2,1,0:T(1,128)S(1)}, s32[1,1,128]{2,1,0:T(1,128)}, u32[]{:S(2)}) copy-start(s32[1,1,128]{2,1,0:T(1,128)} %param.13) | copy-start | bytes 1540
  3.0 33.4 %all-to-all-start = ((bf16[8,1024,128]{2,1,0:T(8,128)(2,1)}), bf16[8,1024,128]{2,1,0:T(8,128)(2,1)S(1)}, u32[]{:S(2)}, u32[]{:S(2)}) async-start(bf16[8,1024,128]{2,1,0:T(8,128)(2,1)} %copies.1), calls=%async_computation | async-start | bytes 4194304 | tf_op jit(solution)/shard_map/all_to_all | solution.py:367
  39.1 4.2 %collective-permute-start = (bf16[8,1024,128]{2,1,0:T(8,128)(2,1)S(1)}, bf16[8,1024,128]{2,1,0:T(8,128)(2,1)S(1)}, u32[]{:S(2)}, u32[]{:S(2)}) collective-permute-start(bf16[8,1024,128]{2,1,0:T(8,128)(2,1)S(1)} %forward_tiles.2), channel_id=1, source_target_pairs={{0,8},{8,0},{16,24},{24,16},{32,40},{40,32},{48,56},{56,48},{64,72... | collective-permute-start | bytes 6291464 | tf_op jit(solution)/shard_map/ppermute | solution.py:359
  43.8 35.5 %copy-start = (bf16[1024,128]{1,0:T(8,128)(2,1)S(1)}, bf16[1024,128]{1,0:T(8,128)(2,1)}, u32[]{:S(2)}) copy-start(bf16[1024,128]{1,0:T(8,128)(2,1)} %cot_ref.1) | copy-start | bytes 786436
  43.8 35.5 %copy-start.1 = (bf16[128,128]{1,0:T(8,128)(2,1)S(1)}, bf16[128,128]{1,0:T(8,128)(2,1)}, u32[]{:S(2)}) copy-start(bf16[128,128]{1,0:T(8,128)(2,1)} %weight_ref.1) | copy-start | bytes 98308
  43.8 35.5 %copy-start.4 = (f32[128]{0:T(128)S(1)}, f32[128]{0:T(128)}, u32[]{:S(2)}) copy-start(f32[128]{0:T(128)} %param.10) | copy-start | bytes 1540
  113.1 4.2 %collective-permute-start.1 = (bf16[8,512,256]{2,1,0:T(8,128)(2,1)S(1)}, bf16[8,512,256]{2,1,0:T(8,128)(2,1)S(1)}, u32[]{:S(2)}, u32[]{:S(2)}) collective-permute-start(bf16[8,512,256]{2,1,0:T(8,128)(2,1)S(1)} %all_to_all.21.g), channel_id=1, source_target_pairs={{0,8},{8,0},{16,24},{24,16},{32,40},{40,32},{48,56},{56,48},{64,72... | collective-permute-start | bytes 6291464 | tf_op jit(solution)/shard_map/ppermute | solution.py:359
  121.0 59.0 %all-to-all-start.3 = ((bf16[8,512,256]{2,1,0:T(8,128)(2,1)}), bf16[8,512,256]{2,1,0:T(8,128)(2,1)S(1)}, u32[]{:S(2)}, u32[]{:S(2)}) async-start(bf16[8,512,256]{2,1,0:T(8,128)(2,1)} %backward_tiles.3), calls=%async_computation.3 | async-start | bytes 4194304 | tf_op jit(solution)/shard_map/all_to_all | solution.py:367
  128.5 24.1 %collective-permute-start.3 = (f32[136,128]{1,0:T(8,128)S(1)}, f32[136,128]{1,0:T(8,128)S(1)}, u32[]{:S(2)}, u32[]{:S(2)}) collective-permute-start(f32[136,128]{1,0:T(8,128)S(1)} %get-tuple-element.16), channel_id=1, source_target_pairs={{0,4},{1,5},{2,6},{3,7},{4,0},{5,1},{6,2},{7,3},{8,12},{9,13},{10,... | collective-permute-start | bytes 208904 | tf_op jit(solution)/shard_map/ppermute | solution.py:371
  132.0 26.7 %collective-permute-start.4 = (f32[136,128]{1,0:T(8,128)S(1)}, f32[136,128]{1,0:T(8,128)S(1)}, u32[]{:S(2)}, u32[]{:S(2)}) collective-permute-start(f32[136,128]{1,0:T(8,128)S(1)} %get-tuple-element.16), channel_id=1, source_target_pairs={{0,6},{1,7},{2,4},{3,5},{4,2},{5,3},{6,0},{7,1},{8,14},{9,15},{10,... | collective-permute-start | bytes 208904 | tf_op jit(solution)/shard_map/ppermute | solution.py:371
  133.1 25.5 %collective-permute-start.2 = (f32[136,128]{1,0:T(8,128)S(1)}, f32[136,128]{1,0:T(8,128)S(1)}, u32[]{:S(2)}, u32[]{:S(2)}) collective-permute-start(f32[136,128]{1,0:T(8,128)S(1)} %get-tuple-element.16), channel_id=1, source_target_pairs={{0,2},{1,3},{2,0},{3,1},{4,6},{5,7},{6,4},{7,5},{8,10},{9,11},{10,... | collective-permute-start | bytes 208904 | tf_op jit(solution)/shard_map/ppermute | solution.py:371
  158.7 1.3 collective-permute-start.5
  160.0 6.0 %collective-permute-start.7 = (f32[136,128]{1,0:T(8,128)S(1)}, f32[136,128]{1,0:T(8,128)S(1)}, u32[]{:S(2)}, u32[]{:S(2)}) collective-permute-start(f32[136,128]{1,0:T(8,128)S(1)} %add.30), channel_id=1, source_target_pairs={{0,16},{8,24},{16,0},{24,8},{32,48},{40,56},{48,32},{56,40},{64,80... | collective-permute-start | bytes 208904 | tf_op jit(solution)/shard_map/ppermute | solution.py:371
  160.1 7.2 %collective-permute-start.8 = (f32[136,128]{1,0:T(8,128)S(1)}, f32[136,128]{1,0:T(8,128)S(1)}, u32[]{:S(2)}, u32[]{:S(2)}) collective-permute-start(f32[136,128]{1,0:T(8,128)S(1)} %add.30), channel_id=1, source_target_pairs={{0,17},{1,16},{2,19},{3,18},{4,21},{5,20},{6,23},{7,22},{8,25},{9,... | collective-permute-start | bytes 208904 | tf_op jit(solution)/shard_map/ppermute | solution.py:394
  164.2 4.3 %collective-permute-start.6 = (f32[136,128]{1,0:T(8,128)S(1)}, f32[136,128]{1,0:T(8,128)S(1)}, u32[]{:S(2)}, u32[]{:S(2)}) collective-permute-start(f32[136,128]{1,0:T(8,128)S(1)} %add.30), channel_id=1, source_target_pairs={{0,1},{1,0},{2,3},{3,2},{4,5},{5,4},{6,7},{7,6},{8,9},{9,8},{10,11... | collective-permute-start | bytes 208904 | tf_op jit(solution)/shard_map/ppermute | solution.py:371
  168.6 4.4 %collective-permute-start.9 = (f32[136,128]{1,0:T(8,128)S(1)}, f32[136,128]{1,0:T(8,128)S(1)}, u32[]{:S(2)}, u32[]{:S(2)}) collective-permute-start(f32[136,128]{1,0:T(8,128)S(1)} %add_add_fusion), channel_id=1, source_target_pairs={{0,32},{8,40},{16,48},{24,56},{32,0},{40,8},{48,16},{56,24},{64,96... | collective-permute-start | bytes 208904 | tf_op jit(solution)/shard_map/ppermute | solution.py:371
  173.0 5.9 %collective-permute-start.10 = (f32[136,128]{1,0:T(8,128)S(1)}, f32[136,128]{1,0:T(8,128)S(1)}, u32[]{:S(2)}, u32[]{:S(2)}) collective-permute-start(f32[136,128]{1,0:T(8,128)S(1)} %add.34), channel_id=1, source_target_pairs={{0,64},{8,72},{16,80},{24,88},{32,96},{40,104},{48,112},{56,120},{... | collective-permute-start | bytes 208904 | tf_op jit(solution)/shard_map/ppermute | solution.py:371
